TPU v7x, 32 devices: a whole 2x2x4 slice. The times are simulated.
32 devices in a mesh: tm: 4 (over z), batch: 8 (over y, x, core).
Axes of the slice: x: 2, y: 2, z: 4, core: 2. Of those that a mesh axis runs over, the one named last changes fastest.
Arguments:
- mel_frames: float32 [24, 512, 512], P('batch', 'tm'), may hold values from -6 to 6
- lengths: int32 [8, 3], P('batch'), may hold values from 1 to 512, 1024 in all within a row
- cotangent: float32 [24, 4096, 256], P('batch', 'tm'), may hold values from -6 to 6
- matrices: float32 [3080192], P(('tm', 'batch')), may hold values from -8 to 8, as said below
- vectors: float32 [3840], P(('tm', 'batch')), may hold values from -3 to 3, as said below
- matrix_first: float32 [3080192], P(('tm', 'batch')), may hold values from -131072 to 131072, as said below
- matrix_second: float32 [3080192], P(('tm', 'batch')), may hold values from 8192 to 65536, as said below
- vector_first: float32 [3840], P(('tm', 'batch')), may hold values from -131072 to 131072, as said below
- vector_second: float32 [3840], P(('tm', 'batch')), may hold values from 8192 to 65536, as said below
Outputs:
- waveform: float32 [24, 4096, 256], P('batch', 'tm')
- frames_grad: float32 [24, 512, 512], P('batch', 'tm')
- new_matrices: float32 [3080192], P(('tm', 'batch'))
- matrix_copy: bfloat16 [3080192], P(('tm', 'batch'))
- matrix_first_new: float32 [3080192], P(('tm', 'batch'))
- matrix_second_new: float32 [3080192], P(('tm', 'batch'))
- new_vectors: float32 [3840], P(('tm', 'batch'))
- vector_copy: bfloat16 [3840], P(('tm', 'batch'))
- vector_first_new: float32 [3840], P(('tm', 'batch'))
- vector_second_new: float32 [3840], P(('tm', 'batch'))
- norm_table: float32 [2, 10], replicated
Inputs may be any that keep to these rules, and one draw needn't show every extreme that they name: `matrices`: entries of both signs, of the size that keeps each layer's output of order one. `vectors`: the gains of the transposed convolution and the shortcuts are positive. `matrix_first`: both signs. `matrix_second`: positive. `vector_first`: both signs. `vector_second`: positive.
All inputs are finite; a program needn't handle non-finite values.
Results may differ from a plain program's by a relative error of at most 0.001.
Values sent between devices are 32-bit elements; how exact they have to be, the bound alone decides.
No kernel may reach another device: no remote copies, remote signals or barrier semaphores. Data moves between devices by JAX's collectives and lax.ppermute only.
A program may use at most 192 MiB of HBM per device.

v0:
```python
import math

import jax
import jax.numpy as jnp
from jax import lax
from jax.sharding import PartitionSpec as P

STEP = 5


B_ONE = 0.5
B_TWO = 0.5
EPSILON = 1e-06
RATE = 0.5
DECAY = 0.01


def with_halo(block, sides, width):
    for axis, dim in sides:
        count = lax.axis_size(axis)
        forward = [(i, i + 1) for i in range(count - 1)]
        backward = [(target, source) for source, target in forward]
        low = lax.ppermute(
            lax.slice_in_dim(block, block.shape[dim] - width, None, axis=dim), axis, forward
        )
        high = lax.ppermute(lax.slice_in_dim(block, 0, width, axis=dim), axis, backward)
        block = jnp.concatenate([low, block, high], axis=dim)
    return block


def matrix_product(left, right):
    return jnp.dot(left, right, precision=lax.Precision.HIGHEST, preferred_element_type=jnp.float32)


def soft_leaky(value):
    return 0.2 * value + 0.8 * jax.nn.softplus(value)


def leaky_slope(value):
    return 0.2 + 0.8 * jax.nn.sigmoid(value)


def layout(in_channels, channels):
    shapes = [(in_channels, 16, channels)]
    for block_position_index in range(3):
        shapes = shapes + [(3, channels, channels), (channels, channels), (channels, channels)]
    starts = []
    position = 0
    for shape in shapes:
        starts.append(position)
        position = position + math.prod(shape)
    return (shapes, starts, position)


def unpack(matrices, vectors, in_channels, channels):
    shapes, starts, whole = layout(in_channels, channels)
    weight_tensors = [
        matrices[first : first + math.prod(shape)].reshape(shape)
        for first, shape in zip(starts, shapes)
    ]
    return (weight_tensors, vectors[:in_channels], vectors[in_channels:].reshape(13, channels))


def moments(gradient, first, second):
    first_new = B_ONE * first + (1.0 - B_ONE) * gradient
    second_new = B_TWO * second + (1.0 - B_TWO) * gradient * gradient
    direction = (
        first_new / (1.0 - B_ONE**STEP) / (jnp.sqrt(second_new / (1.0 - B_TWO**STEP)) + EPSILON)
    )
    return (first_new, second_new, direction)


def forward_rims(value, width):
    return with_halo(value, (("tm", 1),), width)


def backward_rims(value, width):
    return with_halo(value, (("tm", 1),), width)


def body(
    mel_frames,
    lengths,
    cotangent,
    matrices,
    vectors,
    matrix_first,
    matrix_second,
    vector_first,
    vector_second,
):
    segments, frames, in_channels = mel_frames.shape
    channels = cotangent.shape[2]
    sample_values = 8 * frames
    shapes, starts, whole = layout(in_channels, channels)
    local_count = matrices.shape[0]
    owner_place = (
        lax.axis_index("tm") * lax.axis_size("batch") + lax.axis_index("batch")
    ) * local_count
    position = owner_place + jnp.arange(local_count, dtype=jnp.int32)
    lower = jnp.array(starts, jnp.int32)
    upper = jnp.array(starts[1:] + [whole], jnp.int32)
    member = ((position[:, None] >= lower[None, :]) & (position[:, None] < upper[None, :])).astype(
        jnp.float32
    )
    weight_sq = jnp.sum(member * (matrices * matrices)[:, None], axis=0)
    full_mats, full_vecs = (
        lax.all_gather(matrices, ("tm", "batch"), axis=0, tiled=True),
        lax.all_gather(vectors, ("tm", "batch"), axis=0, tiled=True),
    )
    weight_tensors, up_gain, remaining_items = unpack(full_mats, full_vecs, in_channels, channels)
    live = lengths[0]
    frame_pos = lax.axis_index("tm") * frames + jnp.arange(frames, dtype=jnp.int32)
    sample_pos = lax.axis_index("tm") * sample_values + jnp.arange(sample_values, dtype=jnp.int32)
    frame_live = (frame_pos[None, :] < live[:, None]).astype(jnp.float32)
    sample_live = (sample_pos[None, :] < 8 * live[:, None]).astype(jnp.float32)
    masked = mel_frames * frame_live[:, :, None]
    leaky = soft_leaky(masked)
    leaky_rims = with_halo(leaky, (("tm", 1),), 1)
    earlier = leaky_rims[:, :-2].reshape(-1, in_channels)
    following = leaky_rims[:, 2:].reshape(-1, in_channels)
    leaky_flat = leaky.reshape(-1, in_channels)
    up_v = weight_tensors[0]
    up_inv = lax.rsqrt(jnp.sum(up_v * up_v, axis=(1, 2)))
    up_w = up_gain[:, None, None] * up_v * up_inv[:, None, None]
    w_centre = up_w[:, 4:12].reshape(in_channels, 8 * channels)
    w_late = up_w[:, 12:16].reshape(in_channels, 4 * channels)
    w_early = up_w[:, 0:4].reshape(in_channels, 4 * channels)
    centre = matrix_product(leaky_flat, w_centre)
    side = jnp.concatenate(
        [matrix_product(earlier, w_late), matrix_product(following, w_early)], axis=1
    )
    hidden = (centre + side).reshape(-1, channels) + remaining_items[0]
    kept = []
    for block_position_index in range(3):
        dilation_factor = 3**block_position_index
        dilated_weight, pointwise_weight, shortcut_direction = weight_tensors[
            1 + 3 * block_position_index : 4 + 3 * block_position_index
        ]
        dilated_bias, pointwise_bias, shortcut_gain, shortcut_bias = remaining_items[
            1 + 4 * block_position_index : 5 + 4 * block_position_index
        ]
        leaky_input = forward_rims(
            soft_leaky(hidden).reshape(segments, sample_values, channels), dilation_factor
        )
        dilated_output = dilated_bias
        for kernel_offset in range(3):
            window_slice = leaky_input[
                :, kernel_offset * dilation_factor : kernel_offset * dilation_factor + sample_values
            ].reshape(-1, channels)
            dilated_output = dilated_output + matrix_product(
                window_slice, dilated_weight[kernel_offset]
            )
        leaky_mid = soft_leaky(dilated_output)
        branch = pointwise_bias + matrix_product(leaky_mid, pointwise_weight)
        sc_inv = lax.rsqrt(jnp.sum(shortcut_direction * shortcut_direction, axis=0))
        sc_w = shortcut_gain * shortcut_direction * sc_inv
        kept.append((hidden, leaky_input, dilated_output, leaky_mid, sc_inv, sc_w))
        hidden = matrix_product(hidden, sc_w) + shortcut_bias + branch
    waveform = hidden.reshape(segments, sample_values, channels) * sample_live[:, :, None]
    back_flow = (cotangent * sample_live[:, :, None]).reshape(-1, channels)
    block_mats = [None, None, None]
    block_vectors = [None, None, None]
    for block_position_index in (2, 1, 0):
        dilation_factor = 3**block_position_index
        dilated_weight, pointwise_weight, shortcut_direction = weight_tensors[
            1 + 3 * block_position_index : 4 + 3 * block_position_index
        ]
        shortcut_gain = remaining_items[3 + 4 * block_position_index]
        block_in, leaky_input, dilated_output, leaky_mid, sc_inv, sc_w = kept[block_position_index]
        bias_gradient = jnp.sum(back_flow, axis=0)
        pt_grad = matrix_product(leaky_mid.T, back_flow)
        backward_middle = matrix_product(back_flow, pointwise_weight.T) * leaky_slope(
            dilated_output
        )
        dilated_bias_gradient = jnp.sum(backward_middle, axis=0)
        back_pad = backward_rims(
            backward_middle.reshape(segments, sample_values, channels), dilation_factor
        )
        dilated_portions = []
        backward_preceding = jnp.zeros_like(backward_middle)
        for kernel_offset in range(3):
            window_slice = leaky_input[
                :, kernel_offset * dilation_factor : kernel_offset * dilation_factor + sample_values
            ].reshape(-1, channels)
            dilated_portions.append(matrix_product(window_slice.T, backward_middle))
            shifted_input = back_pad[
                :,
                (2 - kernel_offset) * dilation_factor : (2 - kernel_offset) * dilation_factor
                + sample_values,
            ].reshape(-1, channels)
            backward_preceding = backward_preceding + matrix_product(
                shifted_input, dilated_weight[kernel_offset].T
            )
        sc_dir = shortcut_direction * sc_inv
        sc_full = matrix_product(block_in.T, back_flow)
        shortcut_gain_gradient = jnp.sum(sc_full * sc_dir, axis=0)
        sc_v_grad = shortcut_gain * sc_inv * (sc_full - shortcut_gain_gradient * sc_dir)
        block_mats[block_position_index] = [
            jnp.stack(dilated_portions).reshape(-1),
            pt_grad.reshape(-1),
            sc_v_grad.reshape(-1),
        ]
        block_vectors[block_position_index] = [
            dilated_bias_gradient,
            bias_gradient,
            shortcut_gain_gradient,
            bias_gradient,
        ]
        back_flow = backward_preceding * leaky_slope(block_in) + matrix_product(back_flow, sc_w.T)
    up_bias_grad = jnp.sum(back_flow, axis=0)
    up_out = back_flow.reshape(-1, 8 * channels)
    back_frames = backward_rims(back_flow.reshape(segments, sample_values, channels), 8).reshape(
        segments, frames + 2, 8 * channels
    )
    grad_before = back_frames[:, :-2].reshape(-1, 8 * channels)
    grad_after = back_frames[:, 2:].reshape(-1, 8 * channels)
    dw_centre = matrix_product(leaky_flat.T, up_out).reshape(in_channels, 8, channels)
    dw_late = matrix_product(earlier.T, up_out[:, : 4 * channels]).reshape(in_channels, 4, channels)
    dw_early = matrix_product(following.T, up_out[:, 4 * channels :]).reshape(
        in_channels, 4, channels
    )
    up_full = jnp.concatenate([dw_early, dw_centre, dw_late], axis=1)
    back_leaky = (
        matrix_product(up_out, w_centre.T)
        + matrix_product(grad_after[:, : 4 * channels], w_late.T)
        + matrix_product(grad_before[:, 4 * channels :], w_early.T)
    )
    up_dir = up_v * up_inv[:, None, None]
    up_gain_grad = jnp.sum(up_full * up_dir, axis=(1, 2))
    up_v_grad = (
        up_gain[:, None, None]
        * up_inv[:, None, None]
        * (up_full - up_gain_grad[:, None, None] * up_dir)
    )
    frames_grad = (
        back_leaky.reshape(segments, frames, in_channels)
        * leaky_slope(masked)
        * frame_live[:, :, None]
    )
    mat_pieces = [up_v_grad.reshape(-1)]
    vec_pieces = [up_gain_grad, up_bias_grad]
    for block_position_index in range(3):
        mat_pieces = mat_pieces + block_mats[block_position_index]
        vec_pieces = vec_pieces + block_vectors[block_position_index]
    mat_flat = jnp.concatenate(mat_pieces)
    vec_flat = jnp.concatenate(vec_pieces)
    matrix_grad, vector_grad = (
        lax.psum_scatter(mat_flat, ("tm", "batch"), scatter_dimension=0, tiled=True),
        lax.psum_scatter(vec_flat, ("tm", "batch"), scatter_dimension=0, tiled=True),
    )
    matrix_first_new, matrix_second_new, direction = moments(
        matrix_grad, matrix_first, matrix_second
    )
    update = direction + DECAY * matrices
    update_sq = jnp.sum(member * (update * update)[:, None], axis=0)
    weight_sq, update_sq = lax.psum((weight_sq, update_sq), ("tm", "batch"))
    weight_norm = jnp.sqrt(weight_sq)
    update_norm = jnp.sqrt(update_sq)
    trust = weight_norm / update_norm
    entry_trust = jnp.sum(member * trust[None, :], axis=1)
    new_matrices = matrices - RATE * entry_trust * update
    vector_first_new, vector_second_new, vector_step = moments(
        vector_grad, vector_first, vector_second
    )
    new_vectors = vectors - RATE * vector_step
    norm_table = jnp.stack([weight_norm, update_norm])
    return (
        waveform,
        frames_grad,
        new_matrices,
        new_matrices.astype(jnp.bfloat16),
        matrix_first_new,
        matrix_second_new,
        new_vectors,
        new_vectors.astype(jnp.bfloat16),
        vector_first_new,
        vector_second_new,
        norm_table,
    )


def solution(mesh):
    in_specs = (
        P("batch", "tm", None),
        P("batch", None),
        P("batch", "tm", None),
        P(("tm", "batch")),
        P(("tm", "batch")),
        P(("tm", "batch")),
        P(("tm", "batch")),
        P(("tm", "batch")),
        P(("tm", "batch")),
    )
    out_specs = (
        P("batch", "tm", None),
        P("batch", "tm", None),
        P(("tm", "batch")),
        P(("tm", "batch")),
        P(("tm", "batch")),
        P(("tm", "batch")),
        P(("tm", "batch")),
        P(("tm", "batch")),
        P(("tm", "batch")),
        P(("tm", "batch")),
        P(),
    )
    return jax.shard_map(body, mesh=mesh, in_specs=in_specs, out_specs=out_specs, check_vma=False)
```

profile of v0, /device:TPU:0, one launch (start us, length us, event | category | flops | bytes accessed | tf_op | source)
XLA Modules:
  0.0 824.0 jit_solution(3567977293866565934)
XLA Ops:
  11.0 4.9 collective-permute-start
  18.8 42.5 %all-reduce = f32[3840]{0:T(1024)S(1)} all-reduce(f32[3840]{0:T(1024)S(1)} %dynamic-update-slice), channel_id=1, replica_groups=mesh['tm'=4,'batch'=8] {'tm','batch'}, use_global_device_ids=true, to_apply=%add | all-reduce | flops 3840 | bytes 30720
  61.5 47.1 %all-gather.2.cloned.1.call-done = f32[3080192]{0:T(1024)} async-done(((f32[96256]{0:T(1024)}), f32[3080192]{0:T(1024)}) %all-gather.2.cloned.1.call-update) | async-done | bytes 12320784 | tf_op jit(solution)/shard_map/all_gather | solution.py:108
  108.7 5.7 slice.500
  114.4 9.9 %slice.428 = f32[512,16,256]{2,1,0:T(8,128)} reshape(f32[2097152]{0:T(1024)} %slice.500) | data formatting | bytes 16777216 | tf_op jit(solution)/shard_map/slice | solution.py:58
  124.3 4.9 multiply_reduce_fusion.1
  129.1 10.5 %copy.37 = f32[512,16,256]{0,2,1:T(8,128)} copy(f32[512,16,256]{2,1,0:T(8,128)} %slice.428) | data formatting | bytes 16777216 | tf_op jit(solution)/shard_map/slice | solution.py:58
  140.2 4.5 multiply_multiply_fusion
  151.2 7.1 maximum_add_fusion
  161.2 4.6 reshape.482
  165.7 4.0 fusion.102
  177.1 4.0 fusion.13
  182.4 4.7 collective-permute-start.2
  187.1 6.0 fusion.48
  193.1 4.3 convolution_add_fusion.17
  216.4 3.8 pad_maximum_fusion.12
  225.9 6.0 fusion.19
  233.3 4.7 collective-permute-start.4
  238.0 4.3 fusion.95
  251.9 6.1 fusion.23
  259.4 5.0 collective-permute-start.6
  264.4 5.9 fusion.92
  270.3 4.3 convolution_add_fusion.9
  274.7 3.4 pad_maximum_fusion.8
  278.1 5.7 fusion.7
  286.9 4.4 fusion.6
  293.4 6.9 convolution_bitcast_fusion
  303.4 5.7 convolution_bitcast_fusion.1
  309.1 5.1 convolution_bitcast_fusion.3
  314.3 7.0 convolution_bitcast_fusion.2
  321.3 6.0 multiply_reduce_fusion.2
  327.3 4.3 fusion.121
  332.9 4.8 collective-permute-start.9
  343.1 4.8 fusion.122
  347.9 7.0 fusion.5
  355.0 4.7 fusion.117
  359.7 7.3 convolution_bitcast_fusion.4
  367.0 3.3 fusion.116
  370.3 5.3 convolution_bitcast_fusion.5
  375.6 5.2 convolution_bitcast_fusion.7
  380.8 7.1 convolution_bitcast_fusion.6
  387.9 5.3 multiply_reduce_fusion.3
  397.2 5.0 collective-permute-start.11
  411.3 3.4 fusion.3
  417.4 7.0 convolution_bitcast_fusion.8
  424.4 3.3 fusion.114
  427.7 5.4 convolution_bitcast_fusion.9
  433.1 5.2 convolution_bitcast_fusion.11
  438.3 7.4 convolution_bitcast_fusion.10
  445.7 5.1 multiply_reduce_fusion.4
  454.9 4.7 collective-permute-start.13
  465.8 3.6 fusion.1
  469.5 4.3 fusion.113
  487.3 9.3 %fusion.129 = f32[512,8,256]{0,2,1:T(8,128)S(1)} fusion(f32[384,512,1]{1,0,2:T(8,128)} %bitcast.215, f32[8,256,384]{2,1,0:T(8,128)} %bitcast.219), kind=kOutput, calls=%fused_computation.243 | convolution fusion | flops 4831838208 | bytes 8126464 | tf_op jit(solution)/shard_map/dot_general | solution.py:32
  496.7 3.5 fusion.128
  500.3 3.7 fusion.130
  505.2 4.5 subtract_multiply_fusion
  509.8 10.3 %copy.42 = f32[512,16,256]{2,1,0:T(8,128)} copy(f32[512,16,256]{0,2,1:T(8,128)} %subtract_multiply_fusion) | data formatting | bytes 16777216 | tf_op jit(solution)/shard_map/mul | solution.py:232
  520.1 12.2 %copy.43 = f32[1024,2,8,128]{3,1,2,0:T(2,128)S(1)} copy(f32[1024,2,8,128]{3,2,1,0:T(8,128)} %bitcast.190) | data formatting | bytes 16777216
  532.3 3.5 constant_dynamic-update-slice_fusion
  544.7 3.6 collective-permute-start.14
  549.8 7.8 fusion.127
  570.9 199.2 %all-reduce.6.cloned.1.call-done = f32[3080192]{0:T(1024)} async-done(((f32[3080192]{0:T(1024)}), f32[3080192]{0:T(1024)}) %all-reduce.6.cloned.1.call-update) | async-done | bytes 12320784
  773.1 39.8 %all-reduce.3 = (f32[10]{0:T(128)S(1)}, f32[10]{0:T(128)S(1)}, f32[3840]{0:T(1024)S(1)}) all-reduce(f32[10]{0:T(128)S(1)} %get-tuple-element.12, f32[10]{0:T(128)S(1)} %get-tuple-element.11, f32[3840]{0:T(1024)S(1)} %constant_dynamic-update-slice_fusion.11), channel_id=1, replica_groups=mesh['tm'=4,'batch'=8] {'tm','batch'}, use_global_device_ids=true, to_apply=%region_12.13 | all-reduce | flops 3860 | bytes 30880 | tf_op jit(solution)/shard_map/psum | solution.py:257
  (322 shorter events, 148.0 us)
Async XLA Ops:
  7.2 101.5 %all-gather.2.cloned.1.call-start = ((), (), s32[]{:S(2)}) async-start(), calls=%async_computation | async-start | bytes 12705792 | tf_op jit(solution)/shard_map/all_gather | solution.py:108
  7.9 762.2 %all-reduce.6.cloned.1.call-start = ((), (), s32[]{:S(2)}) async-start(), calls=%async_computation.1 | async-start | bytes 24641536
  11.0 140.2 %copy-start.8 = (f32[3,128,512]{2,1,0:T(8,128)}, f32[3,128,512]{2,1,0:T(8,128)S(1)}, u32[]{:S(2)}) copy-start(f32[3,128,512]{2,1,0:T(8,128)S(1)} %fusion.51) | copy-start | bytes 2359300
  11.0 50.3 %collective-permute-start = (f32[3,1,512]{2,1,0:T(1,128)S(1)}, f32[3,1,512]{2,1,0:T(1,128)S(1)}, u32[]{:S(2)}, u32[]{:S(2)}) collective-permute-start(f32[3,1,512]{2,1,0:T(1,128)S(1)} %get-tuple-element.76), channel_id=1, source_target_pairs={{0,8},{8,16},{16,24},{1,9},{9,17},{17,25},{2,10},{10,18},{18,26},{... | collective-permute-start | bytes 18440 | tf_op jit(solution)/shard_map/ppermute | solution.py:23
  16.0 45.3 %collective-permute-start.1 = (f32[3,1,512]{2,1,0:T(1,128)S(1)}, f32[3,1,512]{2,1,0:T(1,128)S(1)}, u32[]{:S(2)}, u32[]{:S(2)}) collective-permute-start(f32[3,1,512]{2,1,0:T(1,128)S(1)} %get-tuple-element.77), channel_id=1, source_target_pairs={{8,0},{16,8},{24,16},{9,1},{17,9},{25,17},{10,2},{18,10},{26,18},{... | collective-permute-start | bytes 18440 | tf_op jit(solution)/shard_map/ppermute | solution.py:26
  61.5 84.1 %copy-start.23 = (f32[3,128,512]{2,1,0:T(8,128)}, f32[3,128,512]{2,1,0:T(8,128)S(1)}, u32[]{:S(2)}) copy-start(f32[3,128,512]{2,1,0:T(8,128)S(1)} %get-tuple-element.75) | copy-start | bytes 2359300
  61.5 86.9 %copy-start.21 = (f32[3,128,512]{2,1,0:T(8,128)}, f32[3,128,512]{2,1,0:T(8,128)S(1)}, u32[]{:S(2)}) copy-start(f32[3,128,512]{2,1,0:T(8,128)S(1)} %get-tuple-element.74) | copy-start | bytes 2359300
  145.1 6.1 copy-start
  145.6 5.6 copy-start.4
  145.6 5.6 copy-start.6
  177.1 10.0 %copy-start.52 = (f32[256,256]{1,0:T(8,128)S(1)}, f32[256,256]{1,0:T(8,128)}, u32[]{:S(2)}) copy-start(f32[256,256]{1,0:T(8,128)} %slice.444) | copy-start | bytes 786436
  181.0 12.1 %copy-start.9 = (f32[3,1024,256]{2,1,0:T(8,128)}, f32[3,1024,256]{2,1,0:T(8,128)S(1)}, u32[]{:S(2)}) copy-start(f32[3,1024,256]{2,1,0:T(8,128)S(1)} %fusion.13) | copy-start | bytes 9437188
  181.1 35.3 %collective-permute-start.3 = (f32[3,1,256]{2,1,0:T(1,128)S(1)}, f32[3,1,256]{2,1,0:T(1,128)S(1)}, u32[]{:S(2)}, u32[]{:S(2)}) collective-permute-start(f32[3,1,256]{2,1,0:T(1,128)S(1)} %get-tuple-element.72), channel_id=1, source_target_pairs={{8,0},{16,8},{24,16},{9,1},{17,9},{25,17},{10,2},{18,10},{26,18},{... | collective-permute-start | bytes 9224 | tf_op jit(solution)/shard_map/ppermute | solution.py:26
  182.4 10.7 %copy-start.19 = (f32[256,256]{1,0:T(8,128)S(1)}, f32[256,256]{1,0:T(8,128)}, u32[]{:S(2)}) copy-start(f32[256,256]{1,0:T(8,128)} %slice.438) | copy-start | bytes 786436
  182.4 34.0 %collective-permute-start.2 = (f32[3,1,256]{2,1,0:T(1,128)S(1)}, f32[3,1,256]{2,1,0:T(1,128)S(1)}, u32[]{:S(2)}, u32[]{:S(2)}) collective-permute-start(f32[3,1,256]{2,1,0:T(1,128)S(1)} %get-tuple-element.73), channel_id=1, source_target_pairs={{0,8},{8,16},{16,24},{1,9},{9,17},{17,25},{2,10},{10,18},{18,26},{... | collective-permute-start | bytes 9224 | tf_op jit(solution)/shard_map/ppermute | solution.py:23
  225.9 6.1 copy-start.39
  225.9 12.1 %copy-start.58 = (f32[256,256]{1,0:T(8,128)S(1)}, f32[256,256]{1,0:T(8,128)}, u32[]{:S(2)}) copy-start(f32[256,256]{1,0:T(8,128)} %slice.458) | copy-start | bytes 786436
  232.0 10.4 %copy-start.10 = (f32[3072,256]{1,0:T(8,128)}, f32[3072,256]{1,0:T(8,128)S(1)}, u32[]{:S(2)}) copy-start(f32[3072,256]{1,0:T(8,128)S(1)} %get-tuple-element.106) | copy-start | bytes 9437188
  232.0 13.2 %collective-permute-start.5 = (f32[3,3,256]{2,1,0:T(4,128)S(1)}, f32[3,3,256]{2,1,0:T(4,128)S(1)}, u32[]{:S(2)}, u32[]{:S(2)}) collective-permute-start(f32[3,3,256]{2,1,0:T(4,128)S(1)} %get-tuple-element.68), channel_id=1, source_target_pairs={{8,0},{16,8},{24,16},{9,1},{17,9},{25,17},{10,2},{18,10},{26,18},{... | collective-permute-start | bytes 27656 | tf_op jit(solution)/shard_map/ppermute | solution.py:26
  233.3 11.9 %collective-permute-start.4 = (f32[3,3,256]{2,1,0:T(4,128)S(1)}, f32[3,3,256]{2,1,0:T(4,128)S(1)}, u32[]{:S(2)}, u32[]{:S(2)}) collective-permute-start(f32[3,3,256]{2,1,0:T(4,128)S(1)} %get-tuple-element.69), channel_id=1, source_target_pairs={{0,8},{8,16},{16,24},{1,9},{9,17},{17,25},{2,10},{10,18},{18,26},{... | collective-permute-start | bytes 27656 | tf_op jit(solution)/shard_map/ppermute | solution.py:23
  251.9 6.1 copy-start.41
  251.9 12.5 %copy-start.61 = (f32[256,256]{1,0:T(8,128)S(1)}, f32[256,256]{1,0:T(8,128)}, u32[]{:S(2)}) copy-start(f32[256,256]{1,0:T(8,128)} %slice.472) | copy-start | bytes 786436
  258.0 6.4 copy-start.29
  258.0 12.3 %copy-start.12 = (f32[3072,256]{1,0:T(8,128)}, f32[3072,256]{1,0:T(8,128)S(1)}, u32[]{:S(2)}) copy-start(f32[3072,256]{1,0:T(8,128)S(1)} %get-tuple-element.108) | copy-start | bytes 9437188
  258.1 16.6 %collective-permute-start.7 = (f32[3,9,256]{2,1,0:T(8,128)S(1)}, f32[3,9,256]{2,1,0:T(8,128)S(1)}, u32[]{:S(2)}, u32[]{:S(2)}) collective-permute-start(f32[3,9,256]{2,1,0:T(8,128)S(1)} %get-tuple-element.64), channel_id=1, source_target_pairs={{8,0},{16,8},{24,16},{9,1},{17,9},{25,17},{10,2},{18,10},{26,18},{... | collective-permute-start | bytes 82952 | tf_op jit(solution)/shard_map/ppermute | solution.py:26
  259.4 15.3 %collective-permute-start.6 = (f32[3,9,256]{2,1,0:T(8,128)S(1)}, f32[3,9,256]{2,1,0:T(8,128)S(1)}, u32[]{:S(2)}, u32[]{:S(2)}) collective-permute-start(f32[3,9,256]{2,1,0:T(8,128)S(1)} %get-tuple-element.65), channel_id=1, source_target_pairs={{0,8},{8,16},{16,24},{1,9},{9,17},{17,25},{2,10},{10,18},{18,26},{... | collective-permute-start | bytes 82952 | tf_op jit(solution)/shard_map/ppermute | solution.py:23
  264.4 5.9 copy-start.16
  278.1 5.8 copy-start.2
  278.1 5.8 copy-start.49
  314.2 7.0 copy-start.17
  321.3 6.0 copy-start.62
  331.6 8.3 %collective-permute-start.8 = (f32[3,9,256]{2,1,0:T(8,128)S(1)}, f32[3,9,256]{2,1,0:T(8,128)S(1)}, u32[]{:S(2)}, u32[]{:S(2)}) collective-permute-start(f32[3,9,256]{2,1,0:T(8,128)S(1)} %get-tuple-element.60), channel_id=1, source_target_pairs={{8,0},{16,8},{24,16},{9,1},{17,9},{25,17},{10,2},{18,10},{26,18},{... | collective-permute-start | bytes 82952 | tf_op jit(solution)/shard_map/ppermute | solution.py:26
  332.9 7.0 collective-permute-start.9
  347.9 7.0 copy-start.18
  359.7 7.3 copy-start.74
  387.9 5.4 copy-start.59
  393.2 8.9 %copy-start.67 = (f32[256,256]{1,0:T(8,128)S(1)}, f32[256,256]{1,0:T(8,128)}, u32[]{:S(2)}) copy-start(f32[256,256]{1,0:T(8,128)} %get-tuple-element.114) | copy-start | bytes 786436
  395.9 10.3 %collective-permute-start.10 = (f32[3,3,256]{2,1,0:T(4,128)S(1)}, f32[3,3,256]{2,1,0:T(4,128)S(1)}, u32[]{:S(2)}, u32[]{:S(2)}) collective-permute-start(f32[3,3,256]{2,1,0:T(4,128)S(1)} %get-tuple-element.56), channel_id=1, source_target_pairs={{8,0},{16,8},{24,16},{9,1},{17,9},{25,17},{10,2},{18,10},{26,18},{... | collective-permute-start | bytes 27656 | tf_op jit(solution)/shard_map/ppermute | solution.py:26
  397.2 9.0 %collective-permute-start.11 = (f32[3,3,256]{2,1,0:T(4,128)S(1)}, f32[3,3,256]{2,1,0:T(4,128)S(1)}, u32[]{:S(2)}, u32[]{:S(2)}) collective-permute-start(f32[3,3,256]{2,1,0:T(4,128)S(1)} %get-tuple-element.57), channel_id=1, source_target_pairs={{0,8},{8,16},{16,24},{1,9},{9,17},{17,25},{2,10},{10,18},{18,26},{... | collective-permute-start | bytes 27656 | tf_op jit(solution)/shard_map/ppermute | solution.py:23
  417.4 7.0 copy-start.72
  438.3 7.4 copy-start.20
  453.6 8.4 %collective-permute-start.12 = (f32[3,1,256]{2,1,0:T(1,128)S(1)}, f32[3,1,256]{2,1,0:T(1,128)S(1)}, u32[]{:S(2)}, u32[]{:S(2)}) collective-permute-start(f32[3,1,256]{2,1,0:T(1,128)S(1)} %get-tuple-element.52), channel_id=1, source_target_pairs={{8,0},{16,8},{24,16},{9,1},{17,9},{25,17},{10,2},{18,10},{26,18},{... | collective-permute-start | bytes 9224 | tf_op jit(solution)/shard_map/ppermute | solution.py:26
  454.9 7.1 collective-permute-start.13
  487.3 9.4 %copy-start.24 = (f32[3,128,512]{2,1,0:T(8,128)S(1)}, f32[3,128,512]{2,1,0:T(8,128)}, u32[]{:S(2)}) copy-start(f32[3,128,512]{2,1,0:T(8,128)} %copy-done.23) | copy-start | bytes 2359300
  487.3 9.4 %copy-start.25 = (f32[1024,384]{1,0:T(8,128)S(1)}, f32[1024,384]{1,0:T(8,128)}, u32[]{:S(2)}) copy-start(f32[1024,384]{1,0:T(8,128)} %copy.38) | copy-start | bytes 4718596
  487.3 16.6 %slice-start = ((s8[8388608]{0:T(1024)(128)(4,1)}), s8[4194304]{0:T(1024)(128)(4,1)S(1)}, s32[]{:S(2)}) async-start(s8[8388608]{0:T(1024)(128)(4,1)} %bitcast.179), calls=%async_computation.2 | async-start | bytes 8388608
  496.7 7.2 slice-start.1
  532.2 5.3 copy-start.68
  535.8 5.8 copy-start.63
  536.8 5.6 copy-start.64
  544.7 12.9 %collective-permute-start.14 = (f32[3,8,256]{2,1,0:T(8,128)S(1)}, f32[3,8,256]{2,1,0:T(8,128)S(1)}, u32[]{:S(2)}, u32[]{:S(2)}) collective-permute-start(f32[3,8,256]{2,1,0:T(8,128)S(1)} %get-tuple-element.48), channel_id=1, source_target_pairs={{0,8},{8,16},{16,24},{1,9},{9,17},{17,25},{2,10},{10,18},{18,26},{... | collective-permute-start | bytes 73736 | tf_op jit(solution)/shard_map/ppermute | solution.py:23
  548.3 9.3 %collective-permute-start.15 = (f32[3,8,256]{2,1,0:T(8,128)S(1)}, f32[3,8,256]{2,1,0:T(8,128)S(1)}, u32[]{:S(2)}, u32[]{:S(2)}) collective-permute-start(f32[3,8,256]{2,1,0:T(8,128)S(1)} %get-tuple-element.49), channel_id=1, source_target_pairs={{8,0},{16,8},{24,16},{9,1},{17,9},{25,17},{10,2},{18,10},{26,18},{... | collective-permute-start | bytes 73736 | tf_op jit(solution)/shard_map/ppermute | solution.py:26
  549.7 7.9 copy-start.1
  566.8 203.3 %copy-start.27 = (f32[96256]{0:T(1024)S(1)}, f32[96256]{0:T(1024)}, u32[]{:S(2)}) copy-start(f32[96256]{0:T(1024)} %param.14) | copy-start | bytes 1155076
  566.8 203.3 %copy-start.69 = (f32[96256]{0:T(1024)S(1)}, f32[96256]{0:T(1024)}, u32[]{:S(2)}) copy-start(f32[96256]{0:T(1024)} %param.16) | copy-start | bytes 1155076
  566.8 203.3 %copy-start.70 = (f32[96256]{0:T(1024)S(1)}, f32[96256]{0:T(1024)}, u32[]{:S(2)}) copy-start(f32[96256]{0:T(1024)} %param.17) | copy-start | bytes 1155076
  569.6 201.9 %copy-start.28 = (s32[96256]{0:T(1024)S(1)}, s32[96256]{0:T(1024)}, u32[]{:S(2)}) copy-start(s32[96256]{0:T(1024)} %iota_add_fusion) | copy-start | bytes 1155076
  569.6 201.8 %copy-start.81 = (s32[10]{0:T(128)S(1)}, s32[10]{0:T(128)}, u32[]{:S(2)}) copy-start(s32[10]{0:T(128)} %constant.60.clone) | copy-start | bytes 124
  569.6 201.8 %copy-start.82 = (s32[10]{0:T(128)S(1)}, s32[10]{0:T(128)}, u32[]{:S(2)}) copy-start(s32[10]{0:T(128)} %constant.59.clone) | copy-start | bytes 124
  570.9 245.4 %copy-start.83 = (f32[120]{0:T(128)S(1)}, f32[120]{0:T(128)}, u32[]{:S(2)}) copy-start(f32[120]{0:T(128)} %param.15) | copy-start | bytes 1444
  570.9 245.4 %copy-start.84 = (f32[120]{0:T(128)S(1)}, f32[120]{0:T(128)}, u32[]{:S(2)}) copy-start(f32[120]{0:T(128)} %param.18) | copy-start | bytes 1444
  570.9 245.4 %copy-start.85 = (f32[120]{0:T(128)S(1)}, f32[120]{0:T(128)}, u32[]{:S(2)}) copy-start(f32[120]{0:T(128)} %param.19) | copy-start | bytes 1444
  771.4 45.5 %copy-start.50 = (f32[96256]{0:T(1024)}, f32[96256]{0:T(1024)S(1)}, u32[]{:S(2)}) copy-start(f32[96256]{0:T(1024)S(1)} %get-tuple-element.25) | copy-start | bytes 1155076
  771.4 45.5 %copy-start.51 = (f32[96256]{0:T(1024)}, f32[96256]{0:T(1024)S(1)}, u32[]{:S(2)}) copy-start(f32[96256]{0:T(1024)S(1)} %get-tuple-element.26) | copy-start | bytes 1155076
  (42 other events, 136.6 us)
Sparse Core Ops, SparseCore 0:
  10.9 97.7 all-gather.1
  543.3 226.8 all-reduce.5
where the time goes:
time: 830 us; the launch traced here: 824 us
  matrix products  253 us (30%)
  waiting for transfers between devices  247 us (30%)
  local copies, waits for them, and re-layouts  127 us (15%)
  blocking collectives  82.2 us (10%)
  other arithmetic  50.8 us (6%)
  starting transfers between devices  47.7 us (6%)
  between operations  16.2 us (2%)
    dot_general x54, matrix products, matrix_product(): jnp.dot(left, right, precision=lax.Precision.HIGHEST, preferred_element_t...  253 us
    unnamed x3, waiting for transfers between devices  200 us
    all_gather x1, waiting for transfers between devices, body(): lax.all_gather(matrices, ('tm', 'batch'), axis=0, tiled=True)  47.1 us
    unnamed x1, blocking collectives  42.5 us
    psum x1, blocking collectives, body(): weight_sq, update_sq = lax.psum((weight_sq, update_sq), ('tm', 'batch'))  39.8 us
    ppermute x8, starting transfers between devices, with_halo(): lax.ppermute(lax.slice_in_dim(block, block.shape[dim] - width, None, axis...  37.3 us
    slice x9, local copies, waits for them, and re-layouts, unpack(): matrices[first:first + math.prod(shape)].reshape(shape)  35 us
    unnamed x210, local copies, waits for them, and re-layouts  34.7 us
  transfers between devices with their start and end apart: 18, of which 2 were waited for; matrix products, arithmetic and copies ran while one was open for 10% of the time, Pallas kernels for 0%

commit v1 on v0

v1 whole, which is shorter than its diff:
```python
import functools
import math

import jax
import jax.numpy as jnp
from jax import lax
from jax.experimental import pallas as pl
from jax.experimental.pallas import tpu as pltpu
from jax.sharding import Mesh
from jax.sharding import PartitionSpec as P

STEP = 5
B_ONE = 0.5
B_TWO = 0.5
EPSILON = 1e-06
RATE = 0.5
DECAY = 0.01
LANES = 128
EDGE_FRAMES = 8
EDGE = 32
PAD = 16
VMEM_LIMIT = 60 * 1024 * 1024
BF16 = jnp.bfloat16
F32 = jnp.float32


def soft_leaky(value):
    small = jnp.exp2(jnp.abs(value) * (-1.0 / math.log(2.0)))
    return jnp.maximum(value, 0.2 * value) + (0.8 * math.log(2.0)) * jnp.log2(1.0 + small)


def leaky_slope(value):
    return 0.6 + 0.4 * jnp.tanh(0.5 * value)


def split(value):
    high = value.astype(BF16)
    return high, (value - high.astype(F32)).astype(BF16)


def cat(parts, axis):
    return jnp.concatenate(parts, axis=axis)


def dot(left, right, dims=((1,), (0,))):
    return lax.dot_general(left, right, (dims, ((), ())), preferred_element_type=F32)


ROWS_COLS = ((1,), (0,))
ROWS_ROWS = ((1,), (1,))
COLS_COLS = ((0,), (0,))


def layout(in_channels, channels):
    shapes = [(in_channels, 16, channels)]
    for _ in range(3):
        shapes = shapes + [(3, channels, channels), (channels, channels), (channels, channels)]
    starts = []
    position = 0
    for shape in shapes:
        starts.append(position)
        position = position + math.prod(shape)
    return (shapes, starts, position)


def start_all(copies):
    for copy in copies:
        copy.start()


def wait_all(copies):
    for copy in copies:
        copy.wait()


def piece_copies(specs, numbers, pieces, flat, vecs, sem, vec_sem, outward):
    copies, vec_copies = [], []
    at = 0

    def move(one, other, signal):
        source, target = (other, one) if outward else (one, other)
        return pltpu.make_async_copy(source, target, signal)

    for spec, piece in zip(specs, pieces):
        for slot in range(spec["slots"]):
            owner = numbers[at]
            first = slot * spec["rows"]
            place = pl.multiple_of(owner * spec["pitch"] + spec["offset"], 8)
            signal = sem.at[at] if outward else sem.at[spec["part"], owner]
            copies.append(
                move(
                    piece.at[pl.ds(first, spec["valid"])],
                    flat.at[pl.ds(place, spec["valid"])],
                    signal,
                )
            )
            if spec["vec"] >= 0:
                place = pl.multiple_of(owner * 8, 8)
                vec_copies.append(
                    move(
                        piece.at[pl.ds(first + spec["vec"], 8)],
                        vecs.at[pl.ds(place, 8)],
                        vec_sem.at[at],
                    )
                )
            at += 1
    return copies, vec_copies


def copy_count(specs):
    return sum(spec["slots"] for spec in specs)


def prepare_kernel(geo, *refs):
    specs, in_ch, ch = geo["specs"], geo["in_ch"], geo["ch"]
    count = len(specs)
    numbers = refs[0]
    pieces = refs[1 : 1 + count]
    given = refs[1 + count : 1 + count + geo["given"]]
    outs = refs[1 + count + geo["given"] :]
    short, inverse, gains, items, squares = outs[6:11]
    flat, scratch, full, sem, vec_sem = outs[11:16]
    up_high, up_low, mat_high, mat_low, turn_high, turn_low = outs[16:22]
    up_sem, mat_sem = outs[22:]

    def up_copies(i):
        span = pl.ds(pl.multiple_of(i * 16, 16), 16)
        pairs = zip(outs[:2], (up_high, up_low))
        return [
            pltpu.make_async_copy(made.at[:, span], out.at[:, span], up_sem.at[n, i])
            for n, (out, made) in enumerate(pairs)
        ]

    def mat_copies(b):
        pairs = zip(outs[2:6], (mat_high, mat_low, turn_high, turn_low))
        return [
            pltpu.make_async_copy(made.at[b], out.at[b], mat_sem.at[n, b])
            for n, (out, made) in enumerate(pairs)
        ]
    vecs = given[0] if geo["given"] else scratch
    copies, vec_copies = piece_copies(specs, numbers, pieces, flat, scratch, sem, vec_sem, False)
    start_all(vec_copies)
    start_all(copies)
    parts = {spec["part"]: spec for spec in specs}
    pitch = specs[0]["pitch"] or flat.shape[0]

    def wait_for(owner):
        for part, spec in parts.items():
            span = pl.ds(0, spec["valid"])
            pltpu.make_async_copy(pieces[0].at[span], flat.at[span], sem.at[part, owner]).wait()

    wait_all(vec_copies)
    full[...] = jnp.zeros_like(full)
    for owner in range(geo["owners"]):
        row = owner * geo["vec_count"] // LANES
        full[row : row + 2] += vecs[8 * owner : 8 * owner + 2]
    columns = full[0:8].T
    gain = cat([columns[:, j : j + 1] for j in range(in_ch // LANES)], 0)
    gains[...] = jnp.broadcast_to(gain, gains.shape)
    items[...] = jnp.zeros_like(items)
    per_row = ch // LANES
    for i in range(13):
        for part in range(per_row):
            row = in_ch // LANES + per_row * i + part
            items[i : i + 1, part * LANES : (part + 1) * LANES] = full[row : row + 1]
    wide = 16 * ch // LANES
    squares[...] = jnp.zeros_like(squares)
    group = 16

    def channels(i, carry):
        first = i * (group * wide)
        now = (first + group * wide - 1) // pitch

        @pl.when((i == 0) | (now > (first - 1) // pitch))
        def _():
            wait_for(now)

        block = flat[pl.ds(pl.multiple_of(first, group * wide), group * wide), :]
        block = jnp.swapaxes(block.reshape(group, wide, LANES), 0, 1)
        square = jnp.sum(block * block, axis=0)
        squares[0:1, :] += jnp.sum(square, axis=0, keepdims=True)
        inv = lax.rsqrt(jnp.sum(square, axis=1, keepdims=True))
        span = pl.ds(pl.multiple_of(i * group, group), group)
        inverse[span, :] = jnp.broadcast_to(inv, (group, LANES))
        scale = gains[span, 0:1] * inv
        for place in range(wide):
            high, low = split(block[place] * scale)
            lanes = slice(place % 2 * LANES, place % 2 * LANES + LANES)
            up_high[place // 2, span, lanes] = high
            up_low[place // 2, span, lanes] = low
        start_all(up_copies(i))
        return carry

    lax.fori_loop(0, in_ch // group, channels, 0)
    for owner in range((in_ch * wide - 1) // pitch + 1, flat.shape[0] // pitch):
        wait_for(owner)
    base = in_ch * wide
    step = ch * ch // LANES
    for block in range(3):
        for number in range(5):
            first = base + (block * 5 + number) * step
            value = cat(
                [flat[pl.ds(first + part, ch, stride=per_row), :] for part in range(per_row)], 1
            )
            column = jnp.sum(value * value, axis=0, keepdims=True)
            which = 1 + 3 * block + max(number - 2, 0)
            squares[which : which + 1, :] += column[:, :LANES] + column[:, LANES:]
            if number == 4:
                short[block, 0:ch] = value
                root = lax.rsqrt(column)
                short[block, ch : ch + 8] = jnp.broadcast_to(root, (8, ch))
                value = value * (items[3 + 4 * block : 4 + 4 * block, :] * root)
            high, low = split(value)
            mat_high[block, number] = high
            mat_low[block, number] = low
            high, low = split(value.T)
            turn_high[block, number] = high
            turn_low[block, number] = low
        start_all(mat_copies(block))

    def finish(i, carry):
        wait_all(up_copies(i))
        return carry

    lax.fori_loop(0, in_ch // group, finish, 0)
    for block in range(3):
        wait_all(mat_copies(block))


def upsample_kernel(
    geo,
    scalars,
    mel_low,
    mel,
    mel_high,
    bias,
    mid_high,
    mid_low,
    side_high,
    side_low,
    out,
    wide,
    mid,
    sides,
):
    segments, frames, ahead = geo["segments"], geo["frames"], geo["ahead"]
    step = pl.program_id(0)
    kept = frames + 2 * (EDGE // 8)
    size = kept + 8
    in_ch = mel.shape[2]

    @pl.when(step == 0)
    def _():
        rows = frames + 2 * EDGE_FRAMES
        wide[...] = jnp.zeros_like(wide)
        place = scalars[segments] * frames - EDGE_FRAMES
        place = place + lax.broadcasted_iota(jnp.int32, (rows, 1), 0)
        inside = ((place >= 0) & (place < ahead)).astype(F32)
        for s in range(segments):
            live = (place < scalars[s]).astype(F32)
            first = 0
            for part in (mel_low, mel, mel_high):
                value = part[s]
                if part is not mel:
                    value = cat([value[0:EDGE_FRAMES], value[EDGE_FRAMES : 2 * EDGE_FRAMES]], 1)
                span = slice(first, first + value.shape[0])
                wide[s, span] = soft_leaky(value * live[span]) * inside[span]
                first = span.stop
        for s in range(segments):
            span = slice(s * size, (s + 1) * size)
            first = EDGE_FRAMES - EDGE // 8
            for target, shift in ((mid, 0), (sides.at[0], -1), (sides.at[1], 1)):
                high, low = split(wide[s, first + shift : first + shift + size])
                target[0, span] = high
                target[1, span] = low

    side = step // 4
    left_high = cat([mid[0], sides[side, 0]], 1)
    left_low = cat([mid[1], sides[side, 1]], 1)
    right_high = cat([mid_high[0], side_high[0]], 0)
    right_low = cat([mid_low[0], side_low[0]], 0)
    value = dot(cat([left_high, left_low, left_high], 1), cat([right_high, right_high, right_low], 0))
    value = value + bias[0:1, :]
    for s in range(segments):
        for half in range(out.shape[1]):
            out[s, half, pl.ds(step, kept, stride=8), :] = value[
                s * size : s * size + kept, half * LANES : (half + 1) * LANES
            ]


def blocks_kernel(
    geo,
    scalars,
    items,
    start,
    cot_low,
    cot,
    cot_high,
    mat_high,
    mat_low,
    turn_high,
    turn_low,
    short,
    wave,
    back,
    grads,
    sums,
    hidden,
    middle,
    padded,
    triple,
    act,
    mid_act,
    hid,
    flow,
    flow_pair,
    dil_acc,
    pair_acc,
):
    segments, ch, samples = geo["segments"], geo["ch"], geo["samples"]
    rows = samples + 2 * EDGE
    count = geo["tiles"]
    tile = rows // count
    tiles = [slice(r, r + tile) for r in range(0, rows, tile)]
    own = slice(EDGE, EDGE + samples)
    segment = pl.program_id(0)
    piece = scalars[segments]
    low_edge = jnp.where(piece > 0, 1.0, 0.0)
    high_edge = jnp.where(piece < scalars[segments + 1] - 1, 1.0, 0.0)
    position = piece * samples - EDGE + lax.broadcasted_iota(jnp.int32, (rows, 1), 0)
    live = position < 8 * scalars[segment]

    @pl.when(segment == 0)
    def _():
        for n in range(2):
            padded[n, 0:PAD] = jnp.zeros((PAD, ch), F32)
            padded[n, PAD + rows : PAD + rows + PAD] = jnp.zeros((PAD, ch), F32)
        dil_acc[...] = jnp.zeros_like(dil_acc)
        pair_acc[...] = jnp.zeros_like(pair_acc)
        sums[...] = jnp.zeros_like(sums)

    def put_padded(n, t, value):
        first, last = PAD + t * tile, PAD + (t + 1) * tile
        if t == 0:
            padded[n, first : first + EDGE] = value[:EDGE] * low_edge
            value, first = value[EDGE:], first + EDGE
        if t == count - 1:
            padded[n, last - EDGE : last] = value[value.shape[0] - EDGE :] * high_edge
            value, last = value[: value.shape[0] - EDGE], last - EDGE
        padded[n, first:last] = value

    def shift(n, t, gap):
        for k in range(3):
            first = PAD + t * tile + (k - 1) * gap
            high, low = split(padded[n, first : first + tile])
            triple[n, 0, tiles[t], k * ch : (k + 1) * ch] = high
            triple[n, 1, tiles[t], k * ch : (k + 1) * ch] = low

    def operand(parts, axis):
        high, low = parts
        return cat([high, high, low] if axis == 0 else [high, low, high], axis)

    def stack(refs, b, numbers):
        return [cat([ref[b, number] for number in numbers], 0) for ref in refs]

    weights = (mat_high, mat_low)
    turned = (turn_high, turn_low)

    def activate(b, t):
        value = hidden[b, tiles[t]]
        put_padded(b % 2, t, soft_leaky(value))
        hid[b, 0, tiles[t]], hid[b, 1, tiles[t]] = split(value)

    def widen(b, t):
        shift(b % 2, t, 3**b)
        act[b, :, tiles[t]] = triple[b % 2, :, tiles[t], ch : 2 * ch]

    def dilated(b, t):
        left = operand([triple[b % 2, n, tiles[t]] for n in range(2)], 1)
        right = operand(stack(weights, b, range(3)), 0)
        middle[b, tiles[t]] = dot(left, right) + items[1 + 4 * b : 2 + 4 * b, :]

    def bend(b, t):
        mid_act[b, 0, tiles[t]], mid_act[b, 1, tiles[t]] = split(soft_leaky(middle[b, tiles[t]]))

    def leave(b, t):
        left = cat(
            [
                operand([mid_act[b, n, tiles[t]] for n in range(2)], 1),
                operand([hid[b, n, tiles[t]] for n in range(2)], 1),
            ],
            1,
        )
        right = cat([operand(stack(weights, b, [number]), 0) for number in (3, 4)], 0)
        offset = items[2 + 4 * b : 3 + 4 * b, :] + items[4 + 4 * b : 5 + 4 * b, :]
        hidden[b + 1, tiles[t]] = dot(left, right) + offset

    for t in range(count):
        hidden[0, tiles[t]] = cat([start[0, half, tiles[t]] for half in range(start.shape[1])], 1)
        activate(0, t)
    for b in range(3):
        for t in range(count + 2):
            if t < count:
                widen(b, t)
                dilated(b, t)
            if 1 <= t <= count:
                bend(b, t - 1)
            if t >= 2:
                leave(b, t - 2)
                if b < 2:
                    activate(b + 1, t - 2)
    wave[0] = jnp.where(live[own], hidden[3, own], 0.0)
    first = 0
    for part in (cot_low[:, 2 * EDGE_FRAMES :], cot, cot_high[:, 2 * EDGE_FRAMES :]):
        span = slice(first, first + part.shape[1])
        flow[span] = jnp.where(live[span], part[0], 0.0)
        first = span.stop

    def part_flow(b, t):
        high, low = split(flow[tiles[t]])
        flow_pair[b % 2, 0, tiles[t]] = high
        flow_pair[b % 2, 1, tiles[t]] = low

    def inner(b, t):
        left = operand([flow_pair[b % 2, n, tiles[t]] for n in range(2)], 1)
        value = dot(left, operand(stack(turned, b, [3]), 0))
        put_padded(b % 2, t, value * leaky_slope(middle[b, tiles[t]]))

    def outer(b, t):
        left = operand([triple[b % 2, n, tiles[t]] for n in range(2)], 1)
        value = dot(left, operand(stack(turned, b, range(3)), 0))
        left = operand([flow_pair[b % 2, n, tiles[t]] for n in range(2)], 1)
        short_part = dot(left, operand(stack(turned, b, [4]), 0))
        flow[tiles[t]] = value * leaky_slope(hidden[b, tiles[t]]) + short_part

    def biases(b):
        body = padded[b % 2, PAD + EDGE : PAD + EDGE + samples]
        sums[8 * b : 8 * b + 1, :] += jnp.sum(body, axis=0, keepdims=True)
        sums[8 * b + 1 : 8 * b + 2, :] += jnp.sum(flow[own], axis=0, keepdims=True)

    def pair_weights(b):
        left = cat([flow_pair[b % 2, n, own].T for n in range(2)], 0)
        right = [cat([mid_act[b, n, own], hid[b, n, own]], 1) for n in range(2)]
        value = dot(left, right[0])
        pair_acc[b] += value[0:ch] + value[ch : 2 * ch] + dot(left[0:ch], right[1])

    def dilated_weights(b):
        left = cat([act[b, n, own].T for n in range(2)], 0)
        value = dot(left, triple[b % 2, 0, own])
        value = value[0:ch] + value[ch : 2 * ch]
        dil_acc[b] += value + dot(left[0:ch], triple[b % 2, 1, own])

    def backward_shift(b, t):
        shift(b % 2, t, -(3**b))

    for t in range(count):
        part_flow(2, t)
    for b in (2, 1, 0):
        for t in range(count):
            inner(b, t)
        pair_weights(b)
        backward_shift(b, 0)
        biases(b)
        for t in range(count):
            if t + 1 < count:
                backward_shift(b, t + 1)
            outer(b, t)
            if b > 0 and t >= 1:
                part_flow(b - 1, t - 1)
        dilated_weights(b)
        if b > 0:
            part_flow(b - 1, count - 1)
    flow[0:EDGE] = flow[0:EDGE] * low_edge
    flow[rows - EDGE : rows] = flow[rows - EDGE : rows] * high_edge
    sums[24:25, :] += jnp.sum(flow[own], axis=0, keepdims=True)
    for half in range(back.shape[1]):
        back[0, half] = flow[:, half * LANES : (half + 1) * LANES]

    @pl.when(segment == segments - 1)
    def _():
        step = ch * ch // LANES
        per_row = ch // LANES

        def put(number, value):
            for part in range(per_row):
                grads[pl.ds(number * step + part, ch, stride=per_row), :] = value[
                    :, part * LANES : (part + 1) * LANES
                ]

        for b in range(3):
            for k in range(3):
                put(5 * b + k, dil_acc[b, :, k * ch : (k + 1) * ch])
            put(5 * b + 3, pair_acc[b, :, 0:ch].T)
            whole = pair_acc[b, :, ch : 2 * ch].T
            inv = short[b, ch : ch + 1]
            direction = short[b, 0:ch] * inv
            along = jnp.sum(whole * direction, axis=0, keepdims=True)
            sums[8 * b + 2 : 8 * b + 3, :] = along
            gain = items[3 + 4 * b : 4 + 4 * b, :]
            put(5 * b + 4, gain * inv * (whole - along * direction))


def tap_window(back, tap, segments, frames):
    first = EDGE - 4 + tap
    halves = range(back.shape[1])
    return cat(
        [
            cat([back[s, half, pl.ds(first, frames, stride=8), :] for half in halves], 1)
            for s in range(segments)
        ],
        0,
    )


def weight_back_kernel(geo, scalars, numbers, mel, gain, inverse, sums, back, high, low, blocks, *refs):
    specs, segments, frames = geo["specs"], geo["segments"], geo["frames"]
    count = len(specs)
    pieces = refs[:count]
    outs = refs[count:]
    extra = outs[0] if geo["given"] else None
    turned, whole, kept, slope, flat, scratch, full, block_sem, sem, vec_sem = outs[
        geo["given"] :
    ]
    vecs = extra if geo["given"] else scratch
    step = pl.program_id(0)
    taps = pl.num_programs(0)
    in_ch = mel.shape[2]
    ch = high.shape[2]
    wide = 16 * ch // LANES
    body = in_ch * wide
    loads = [
        pltpu.make_async_copy(blocks, flat.at[pl.ds(body, blocks.shape[0])], block_sem.at[0]),
        pltpu.make_async_copy(high, kept.at[0], block_sem.at[1]),
        pltpu.make_async_copy(low, kept.at[1], block_sem.at[2]),
    ]

    @pl.when(step == 0)
    def _():
        start_all(loads)
        place = scalars[segments] * frames + lax.broadcasted_iota(jnp.int32, (frames, 1), 0)
        for s in range(segments):
            live = (place < scalars[s]).astype(F32)
            upper, lower = split(soft_leaky(mel[s] * live).T)
            for part, piece in enumerate((upper, lower, upper)):
                first = (part * segments + s) * frames
                turned[:, first : first + frames] = piece

    upper, lower = split(tap_window(back, step, segments, frames))
    whole[step] = dot(turned[...], cat([upper, upper, lower], 0))

    @pl.when(step == taps - 1)
    def _():
        wait_all(loads)
        group = 16

        def channels(i, carry):
            span = pl.ds(pl.multiple_of(i * group, group), group)
            along = jnp.zeros((group, ch), F32)
            for tap in range(16):
                raw = kept[0, tap, span].astype(F32) + kept[1, tap, span].astype(F32)
                along = along + raw * whole[tap, span]
            factor = gain[span, 0:1]
            column = jnp.sum(along, axis=1, keepdims=True) / factor
            slope[span] = jnp.broadcast_to(column, (group, LANES))
            inv = inverse[span, 0:1]
            scale = factor * inv
            turn = inv * column
            values = []
            for tap in range(16):
                raw = kept[0, tap, span].astype(F32) + kept[1, tap, span].astype(F32)
                value = scale * whole[tap, span] - turn * raw
                for half in range(ch // LANES):
                    values.append(value[:, half * LANES : (half + 1) * LANES])
            block = jnp.swapaxes(jnp.stack(values), 0, 1).reshape(group * wide, LANES)
            flat[pl.ds(pl.multiple_of(i * (group * wide), group * wide), group * wide), :] = block
            return carry

        lax.fori_loop(0, in_ch // group, channels, 0)
        for j in range(in_ch // LANES):
            full[j : j + 1] = slope[j * LANES : (j + 1) * LANES].T[0:1]
        order = [24]
        for b in range(3):
            order += [8 * b, 8 * b + 1, 8 * b + 2, 8 * b + 1]
        row = in_ch // LANES
        for number in order:
            for part in range(ch // LANES):
                full[row : row + 1] = sums[number : number + 1, part * LANES : (part + 1) * LANES]
                row += 1
        vecs[...] = jnp.zeros_like(vecs)
        for owner in range(geo["owners"]):
            row = owner * geo["vec_count"] // LANES
            vecs[8 * owner : 8 * owner + 2] = full[row : row + 2]

        copies, vec_copies = piece_copies(
            specs, numbers, pieces, flat, scratch, sem, vec_sem, True
        )
        start_all(copies + vec_copies)
        wait_all(copies + vec_copies)


def frames_back_kernel(geo, scalars, mel, back, high, low, out, total):
    segments, frames = geo["segments"], geo["frames"]
    step = pl.program_id(0)

    @pl.when(step == 0)
    def _():
        total[...] = jnp.zeros_like(total)

    upper, lower = split(tap_window(back, step, segments, frames))
    total[...] += dot(
        cat([upper, lower, upper], 1), cat([high[0], high[0], low[0]], 1), ROWS_ROWS
    )

    @pl.when(step == pl.num_programs(0) - 1)
    def _():
        place = scalars[segments] * frames + lax.broadcasted_iota(jnp.int32, (frames, 1), 0)
        for s in range(segments):
            live = (place < scalars[s]).astype(F32)
            value = total[s * frames : (s + 1) * frames]
            out[s] = value * leaky_slope(mel[s] * live) * live


def whole_spec(shape):
    return pl.BlockSpec(shape, lambda *_: (0,) * len(shape))


def vmem():
    return pl.BlockSpec(memory_space=pltpu.VMEM)


def smem():
    return pl.BlockSpec(memory_space=pltpu.SMEM)


def anywhere():
    return pl.BlockSpec(memory_space=pl.ANY)


def shape(dims, dtype=F32):
    return jax.ShapeDtypeStruct(dims, dtype)


def params():
    return pltpu.CompilerParams(vmem_limit_bytes=VMEM_LIMIT)


def prepare(pieces, specs, numbers, given, geo):
    in_ch, ch = geo["in_ch"], geo["ch"]
    entries = (in_ch * 16 * ch + 15 * ch * ch) // LANES
    geo = dict(geo, specs=specs, given=len(given))
    return pl.pallas_call(
        functools.partial(prepare_kernel, geo),
        out_shape=(
            shape((16, in_ch, ch), BF16),
            shape((16, in_ch, ch), BF16),
            shape((3, 5, ch, ch), BF16),
            shape((3, 5, ch, ch), BF16),
            shape((3, 5, ch, ch), BF16),
            shape((3, 5, ch, ch), BF16),
            shape((3, ch + 8, ch)),
            shape((in_ch, LANES)),
            shape((in_ch, LANES)),
            shape((16, ch)),
            shape((16, LANES)),
        ),
        in_specs=[smem()] + [anywhere()] * len(pieces) + [vmem()] * len(given),
        out_specs=(anywhere(),) * 6 + (vmem(),) * 5,
        scratch_shapes=[
            pltpu.VMEM((entries, LANES), F32),
            pltpu.VMEM((8 * geo["owners"], LANES), F32),
            pltpu.VMEM((40, LANES), F32),
            pltpu.SemaphoreType.DMA((3, geo["owners"])),
            pltpu.SemaphoreType.DMA((copy_count(specs),)),
            pltpu.VMEM((16, in_ch, ch), BF16),
            pltpu.VMEM((16, in_ch, ch), BF16),
        ]
        + [pltpu.VMEM((3, 5, ch, ch), BF16)] * 4
        + [
            pltpu.SemaphoreType.DMA((2, in_ch // 16)),
            pltpu.SemaphoreType.DMA((4, 3)),
        ],
        compiler_params=params(),
    )(numbers, *pieces, *given)


def upsample(scalars, mel_parts, items, up_high, up_low, ahead):
    segments, frames, in_ch = mel_parts[1].shape
    ch = up_high.shape[2]
    kept = frames + 2 * (EDGE // 8)
    size = kept + 8
    geo = {"segments": segments, "frames": frames, "ahead": ahead}
    out = (segments, ch // LANES, 8 * kept, LANES)
    return pl.pallas_call(
        functools.partial(upsample_kernel, geo),
        grid=(8,),
        out_shape=shape(out),
        in_specs=[smem()]
        + [whole_spec(part.shape) for part in mel_parts]
        + [
            whole_spec(items.shape),
            pl.BlockSpec((1, in_ch, ch), lambda j: (j + 4, 0, 0)),
            pl.BlockSpec((1, in_ch, ch), lambda j: (j + 4, 0, 0)),
            pl.BlockSpec((1, in_ch, ch), lambda j: ((j + 12) % 16, 0, 0)),
            pl.BlockSpec((1, in_ch, ch), lambda j: ((j + 12) % 16, 0, 0)),
        ],
        out_specs=whole_spec(out),
        scratch_shapes=[
            pltpu.VMEM((segments, frames + 2 * EDGE_FRAMES + 16, in_ch), F32),
            pltpu.VMEM((2, segments * size, in_ch), BF16),
            pltpu.VMEM((2, 2, segments * size, in_ch), BF16),
        ],
        compiler_params=params(),
    )(scalars, *mel_parts, items, up_high, up_low, up_high, up_low)


def blocks(scalars, items, start, cot_parts, mat_high, mat_low, turn_high, turn_low, short):
    segments, samples, ch = cot_parts[1].shape
    rows = samples + 2 * EDGE
    geo = {"segments": segments, "samples": samples, "ch": ch, "tiles": 4}
    halves = start.shape[1]
    flat = (15 * ch * ch // LANES, LANES)
    once = pl.Buffered(1)

    def fixed(dims):
        return pl.BlockSpec(dims, lambda s: (0,) * len(dims), pipeline_mode=once)

    return pl.pallas_call(
        functools.partial(blocks_kernel, geo),
        grid=(segments,),
        out_shape=(
            shape((segments, samples, ch)),
            shape((segments, halves, rows, LANES)),
            shape(flat),
            shape((32, ch)),
        ),
        in_specs=[
            smem(),
            fixed(items.shape),
            pl.BlockSpec((1, halves, rows, LANES), lambda s: (s, 0, 0, 0)),
        ]
        + [pl.BlockSpec((1,) + part.shape[1:], lambda s: (s, 0, 0)) for part in cot_parts]
        + [
            fixed(mat_high.shape),
            fixed(mat_low.shape),
            fixed(turn_high.shape),
            fixed(turn_low.shape),
            fixed(short.shape),
        ],
        out_specs=(
            pl.BlockSpec((1, samples, ch), lambda s: (s, 0, 0)),
            pl.BlockSpec((1, halves, rows, LANES), lambda s: (s, 0, 0, 0)),
            pl.BlockSpec(flat, lambda s: (0, 0), pipeline_mode=once),
            pl.BlockSpec((32, ch), lambda s: (0, 0)),
        ),
        scratch_shapes=[
            pltpu.VMEM((4, rows, ch), F32),
            pltpu.VMEM((3, rows, ch), F32),
            pltpu.VMEM((2, rows + 2 * PAD, ch), F32),
            pltpu.VMEM((2, 2, rows, 3 * ch), BF16),
            pltpu.VMEM((3, 2, rows, ch), BF16),
            pltpu.VMEM((3, 2, rows, ch), BF16),
            pltpu.VMEM((3, 2, rows, ch), BF16),
            pltpu.VMEM((rows, ch), F32),
            pltpu.VMEM((2, 2, rows, ch), BF16),
            pltpu.VMEM((3, ch, 3 * ch), F32),
            pltpu.VMEM((3, ch, 2 * ch), F32),
        ],
        compiler_params=params(),
    )(scalars, items, start, *cot_parts, mat_high, mat_low, turn_high, turn_low, short)


def weight_back(scalars, mel, gain, inverse, sums, back, high, low, block_grads, specs, numbers, geo):
    segments, frames, in_ch = mel.shape
    ch = high.shape[2]
    body = in_ch * 16 * ch // LANES
    given = 0 if specs[-1]["vec"] >= 0 else 1
    geo = dict(geo, specs=specs, segments=segments, frames=frames, given=given)
    vec_shape = (8 * geo["owners"], LANES)
    return pl.pallas_call(
        functools.partial(weight_back_kernel, geo),
        grid=(16,),
        out_shape=tuple(shape((spec["slots"] * spec["rows"], LANES)) for spec in specs)
        + (shape(vec_shape),) * given,
        in_specs=[
            smem(),
            smem(),
            whole_spec(mel.shape),
            whole_spec(gain.shape),
            whole_spec(inverse.shape),
            whole_spec(sums.shape),
            whole_spec(back.shape),
            anywhere(),
            anywhere(),
            anywhere(),
        ],
        out_specs=(anywhere(),) * len(specs) + (whole_spec(vec_shape),) * given,
        scratch_shapes=[
            pltpu.VMEM((in_ch, 3 * segments * frames), BF16),
            pltpu.VMEM((16, in_ch, ch), F32),
            pltpu.VMEM((2, 16, in_ch, ch), BF16),
            pltpu.VMEM((in_ch, LANES), F32),
            pltpu.VMEM((body + block_grads.shape[0], LANES), F32),
            pltpu.VMEM(vec_shape, F32),
            pltpu.VMEM((40, LANES), F32),
            pltpu.SemaphoreType.DMA((3,)),
            pltpu.SemaphoreType.DMA((copy_count(specs),)),
            pltpu.SemaphoreType.DMA((copy_count(specs),)),
        ],
        compiler_params=params(),
    )(scalars, numbers, mel, gain, inverse, sums, back, high, low, block_grads)


def frames_back(scalars, mel, back, high, low):
    segments, frames, in_ch = mel.shape
    ch = high.shape[2]
    geo = {"segments": segments, "frames": frames}
    weight = pl.BlockSpec((1, in_ch, ch), lambda k: (k, 0, 0))
    return pl.pallas_call(
        functools.partial(frames_back_kernel, geo),
        grid=(16,),
        out_shape=shape(mel.shape),
        in_specs=[smem(), whole_spec(mel.shape), whole_spec(back.shape), weight, weight],
        out_specs=whole_spec(mel.shape),
        scratch_shapes=[pltpu.VMEM((segments * frames, in_ch), F32)],
        compiler_params=params(),
        cost_estimate=pl.CostEstimate(
            flops=6 * segments * frames * in_ch * 16 * ch,
            bytes_accessed=4 * 16 * in_ch * ch + 8 * mel.size + 4 * back.size,
            transcendentals=0,
        ),
    )(scalars, mel, back, high, low)


def line_edges(low, high, axis):
    count = math.prod(lax.axis_size(name) for name in axis)
    forward = [(i, i + 1) for i in range(count - 1)]
    backward = [(target, source) for source, target in forward]
    return lax.ppermute(high, axis, forward), lax.ppermute(low, axis, backward)


def packed_edges(mel, cot):
    ch = cot.shape[2]
    edges = []
    for frames, samples in (
        (mel[:, :EDGE_FRAMES], cot[:, :EDGE]),
        (mel[:, mel.shape[1] - EDGE_FRAMES :], cot[:, cot.shape[1] - EDGE :]),
    ):
        edges.append(cat([frames[:, :, :ch], frames[:, :, ch:], samples], 1))
    return edges


def moments(gradient, first, second):
    first_new = B_ONE * first + (1.0 - B_ONE) * gradient
    second_new = B_TWO * second + (1.0 - B_TWO) * gradient * gradient
    direction = (
        first_new / (1.0 - B_ONE**STEP) / (jnp.sqrt(second_new / (1.0 - B_TWO**STEP)) + EPSILON)
    )
    return (first_new, second_new, direction)


def total(value, axes):
    for axis in axes:
        count = lax.axis_size(axis)
        step = 1
        while step < count:
            value = value + lax.ppermute(value, axis, [(i, i ^ step) for i in range(count)])
            step = 2 * step
    return value


FLIPS = {"wide": ("wide", 1), "deep": ("deep", 1), "near": ("line", 1), "far": ("line", 2), "core": ("core", 1)}
ORDERS = (("wide", "deep", "near", "far"), ("deep", "wide", "near", "far"), ("near", "far", "wide", "deep"))
LANE_ROWS = 8


def swap(value, flip):
    axis, step = FLIPS[flip]
    return lax.ppermute(value, axis, [(i, i ^ step) for i in range(lax.axis_size(axis))])


def owner_table(order, other_core):
    places = {name: lax.axis_index(name) for name in ("line", "deep", "wide", "core")}
    numbers = []
    for slot in range(16):
        here = dict(places)
        for bit, flip in enumerate(order):
            if slot >> (3 - bit) & 1:
                axis, step = FLIPS[flip]
                here[axis] = here[axis] ^ step
        core = here["core"] ^ other_core
        numbers.append(((here["line"] * 2 + here["deep"]) * 2 + here["wide"]) * 2 + core)
    return jnp.stack(numbers).astype(jnp.int32)


def part_sizes(shard_rows):
    last = shard_rows * 7 // 48 // 8 * 8
    first = (shard_rows - last) // 16 * 8
    return (first, first, shard_rows - 2 * first)


def part_specs(sizes, rows, slots):
    specs = []
    offset = 0
    for part, size in enumerate(sizes):
        valid = min(size, rows - offset)
        specs.append(
            {
                "part": part,
                "slots": slots,
                "rows": size,
                "pitch": rows,
                "offset": offset,
                "valid": valid,
                "vec": valid if valid < size else -1,
            }
        )
        offset += size
    return specs


def together(*values):
    return lax.optimization_barrier(values)


def gather_by_permutes(shard, sizes, edges, tm):
    first, second, third = sizes
    both, last = shard[: first + second], shard[first + second :]
    far, near, last_deep, last_wide, edges = together(
        swap(both, "far"),
        swap(both, "near"),
        swap(last, "deep"),
        swap(last, "wide"),
        line_edges(*edges, tm),
    )
    near_far, last_both = together(swap(far, "near"), swap(last_deep, "wide"))
    parts = (both, far, near, near_far)
    a = cat([part[:first] for part in parts], 0)
    b = cat([part[first:] for part in parts], 0)
    c = cat([last, last_deep, last_wide, last_both], 0)
    a, b, c = together(a, b, c)
    a_deep, b_wide, c_far = swap(a, "deep"), swap(b, "wide"), swap(c, "far")
    c_near = swap(c, "near")
    a_deep, b_wide, c_far, c_near, a, b = together(a_deep, b_wide, c_far, c_near, a, b)
    c_both = swap(c_far, "near")
    a_both, b_both = swap(a_deep, "wide"), swap(b_wide, "deep")
    a_wide, b_deep = swap(a, "wide"), swap(b, "deep")
    ready = [(0, 0, a), (1, 0, b), (2, 0, c), (0, 1, a_deep), (1, 1, b_wide), (2, 1, c_far)]
    ready.append((2, 2, c_near))
    others = [swap(array, "core") for _, _, array in ready]
    a_both, b_both, a_wide, b_deep, c_both, others = together(
        a_both, b_both, a_wide, b_deep, c_both, others
    )
    held = [(n, quarter, 0, array) for n, quarter, array in ready]
    held += [(n, quarter, 1, array) for (n, quarter, _), array in zip(ready, others)]
    rest = [(0, 2, a_wide), (1, 2, b_deep), (0, 3, a_both), (1, 3, b_both), (2, 3, c_both)]
    for n, quarter, array in rest:
        held += [(n, quarter, 0, array), (n, quarter, 1, swap(array, "core"))]
    return held, edges


def scatter_by_permutes(mine, theirs, sizes, beside):
    came = together(*[swap(value, "core") for value in theirs])
    terms = [[own, other] for own, other in zip(mine, came)]
    slots = 16
    for level in range(4):
        slots = slots // 2
        away = []
        for part, size in zip(terms, sizes):
            away.append(sum(term[slots * size : 2 * slots * size] for term in part))
        came = [swap(value, order[level]) for value, order in zip(away, ORDERS)]
        if level == 0:
            came, other = together(came, beside())
        else:
            came = together(*came)
        for part, value in zip(terms, came):
            part.append(value)
    summed = cat([sum(term[:size] for term in part) for part, size in zip(terms, sizes)], 0)
    return summed, other


def by_owner(mine, theirs, plan):
    grid, core_dim = plan["grid"], plan["core_dim"]
    first = lax.axis_index("core") == 0
    parts = [jnp.where(first, mine, theirs), jnp.where(first, theirs, mine)]
    chips = [size for place, size in enumerate(grid) if place != core_dim]
    parts = [part.reshape(chips + list(mine.shape[1:])) for part in parts]
    return jnp.stack(parts, axis=core_dim).reshape((-1,) + mine.shape[1:])


def by_core(shards, plan):
    grid, core_dim = plan["grid"], plan["core_dim"]
    grouped = shards.reshape(tuple(grid) + shards.shape[1:])
    core = lax.axis_index("core")
    mine = lax.dynamic_index_in_dim(grouped, core, core_dim, keepdims=False)
    theirs = lax.dynamic_index_in_dim(grouped, 1 - core, core_dim, keepdims=False)
    after = (-1,) + shards.shape[1:]
    return mine.reshape(after), theirs.reshape(after)


def body(
    plan,
    mel_frames,
    lengths,
    cotangent,
    matrices,
    vectors,
    matrix_first,
    matrix_second,
    vector_first,
    vector_second,
):
    tm, every, chip_axes = plan["tm"], plan["every"], plan["chip_axes"]
    segments, frames, in_ch = mel_frames.shape
    ch = cotangent.shape[2]
    pieces = math.prod(lax.axis_size(name) for name in tm)
    rows = matrices.shape[0] // LANES
    shard_rows = -(-(rows + 2) // 48) * 48
    vec_count = vectors.shape[0]
    spare = shard_rows - rows - 2
    owners = math.prod(plan["grid"])
    geo = {"in_ch": in_ch, "ch": ch, "owners": owners, "vec_count": vec_count}
    vec_first = lax.axis_index(every) * vec_count % LANES
    placed = lax.dynamic_update_slice(jnp.zeros((2 * LANES,), F32), vectors, (vec_first,))
    shard = jnp.concatenate(
        [
            matrices.reshape(rows, LANES),
            placed.reshape(2, LANES),
            jnp.zeros((spare, LANES), F32),
        ]
    )
    edges = packed_edges(mel_frames, cotangent)
    cubic = rows % 8 == 0 and plan["grid"] == (4, 2, 2, 2)
    sizes = part_sizes(shard_rows)
    if cubic:
        specs = part_specs(sizes, rows, 16)
        numbers = [[owner_table(order, core) for order in ORDERS] for core in range(2)]
        held, edges = gather_by_permutes(shard, sizes, edges, tm)
        held_numbers = jnp.concatenate(
            [numbers[c][n][4 * quarter : 4 * quarter + 4] for n, quarter, c, _ in held]
        )
        held_specs = [dict(specs[n], slots=4) for n, _, _, _ in held]
        held = [array for _, _, _, array in held]
        given = []
    else:
        edges = line_edges(*edges, tm)
        mine = lax.all_gather(shard, chip_axes, axis=0, tiled=False)
        gathered = by_owner(mine, swap(mine, "core"), plan)
        held = [gathered[:, :rows].reshape(-1, LANES)]
        whole = held[0].shape[0]
        specs = [
            {
                "part": 0,
                "slots": 1,
                "rows": whole,
                "pitch": 0,
                "offset": 0,
                "valid": whole,
                "vec": -1,
            }
        ]
        held_specs, held_numbers = specs, jnp.zeros((1,), jnp.int32)
        vec_rows = jnp.pad(gathered[:, rows : rows + 2], ((0, 0), (0, LANE_ROWS - 2), (0, 0)))
        given = [vec_rows.reshape(-1, LANES)]
    mel_parts = (edges[0], mel_frames, edges[1])
    cot_parts = (edges[0], cotangent, edges[1])
    scalars = jnp.concatenate(
        [lengths[0], jnp.stack([lax.axis_index(tm), jnp.int32(pieces)]).astype(jnp.int32)]
    )
    up_high, up_low, *mats, short, inverse, gain, items, squares = prepare(
        held, held_specs, held_numbers, given, geo
    )
    start = upsample(scalars, mel_parts, items, up_high, up_low, pieces * frames)
    waveform, back, block_grads, sums = blocks(scalars, items, start, cot_parts, *mats, short)
    if cubic:
        out_specs = specs * 2
        out_numbers = jnp.concatenate(numbers[0] + numbers[1])
    else:
        out_specs, out_numbers = held_specs, held_numbers
    grads = weight_back(
        scalars,
        mel_frames,
        gain,
        inverse,
        sums,
        back,
        up_high,
        up_low,
        block_grads,
        out_specs,
        out_numbers,
        geo,
    )
    if cubic:
        summed, frames_grad = scatter_by_permutes(
            grads[:3],
            grads[3:],
            sizes,
            lambda: frames_back(scalars, mel_frames, back, up_high, up_low),
        )
    else:
        vec_rows = grads[1].reshape(owners, LANE_ROWS, LANES)[:, :2]
        shards = jnp.concatenate(
            [
                grads[0].reshape(owners, rows, LANES),
                vec_rows,
                jnp.zeros((owners, spare, LANES), F32),
            ],
            axis=1,
        )
        mine, theirs = by_core(shards, plan)
        mine = mine + swap(theirs, "core")
        summed = lax.psum_scatter(mine, chip_axes, scatter_dimension=0, tiled=True)[0]
        frames_grad = frames_back(scalars, mel_frames, back, up_high, up_low)
    matrix_grad = summed[:rows]
    vec_rows = summed[rows : rows + 2].reshape(-1)
    vector_grad = lax.dynamic_slice(vec_rows, (vec_first,), (vec_count,))

    shapes, starts, whole = layout(in_ch, ch)
    matrices = matrices.reshape(rows, LANES)
    position = lax.axis_index(every) * rows + jnp.arange(rows, dtype=jnp.int32)
    lower = jnp.array([first // LANES for first in starts], jnp.int32)
    upper = jnp.array([first // LANES for first in starts[1:] + [whole]], jnp.int32)
    member = (position[:, None] >= lower[None, :]) & (position[:, None] < upper[None, :])
    member = member.astype(F32)
    matrix_first_new, matrix_second_new, direction = moments(
        matrix_grad, matrix_first.reshape(rows, LANES), matrix_second.reshape(rows, LANES)
    )
    update = direction + DECAY * matrices
    update_sq = jnp.sum(member * jnp.sum(update * update, axis=1)[:, None], axis=0)
    update_sq = total(update_sq, every)
    weight_norm = jnp.sqrt(jnp.sum(squares[:10], axis=1))
    update_norm = jnp.sqrt(update_sq)
    trust = weight_norm / update_norm
    row_trust = jnp.sum(member * trust[None, :], axis=1)
    new_matrices = (matrices - RATE * row_trust[:, None] * update).reshape(-1)
    vector_first_new, vector_second_new, vector_step = moments(
        vector_grad, vector_first, vector_second
    )
    new_vectors = vectors - RATE * vector_step
    norm_table = jnp.stack([weight_norm, update_norm])
    return (
        waveform,
        frames_grad,
        new_matrices,
        new_matrices.astype(BF16),
        matrix_first_new.reshape(-1),
        matrix_second_new.reshape(-1),
        new_vectors,
        new_vectors.astype(BF16),
        vector_first_new,
        vector_second_new,
        norm_table,
    )


def make_plan(mesh):
    tm, batch = mesh.shape["tm"], mesh.shape["batch"]
    if tm > 4:
        root = math.isqrt(batch)
        grid = (tm // 2, 2, root, batch // root)
        names = ("line", "core", "deep", "wide")
        tm_axes, batch_axes = ("line", "core"), ("deep", "wide")
        core_dim = 1
    else:
        root = math.isqrt(batch // 2)
        grid = (tm, root, batch // 2 // root, 2)
        names = ("line", "deep", "wide", "core")
        tm_axes, batch_axes = ("line",), ("deep", "wide", "core")
        core_dim = 3
    inner = Mesh(mesh.devices.reshape(grid), names)
    plan = {
        "tm": tm_axes,
        "batch": batch_axes,
        "every": names,
        "grid": grid,
        "core_dim": core_dim,
        "chip_axes": tuple(name for name in names if name != "core"),
    }
    return inner, plan


def solution(mesh):
    inner, plan = make_plan(mesh)
    tm, batch, every = plan["tm"], plan["batch"], plan["every"]
    pieces, flat = P(batch, tm, None), P(every)
    in_specs = (pieces, P(batch, None), pieces, flat, flat, flat, flat, flat, flat)
    out_specs = (pieces, pieces, flat, flat, flat, flat, flat, flat, flat, flat, P())
    return jax.shard_map(
        functools.partial(body, plan),
        mesh=inner,
        in_specs=in_specs,
        out_specs=out_specs,
        check_vma=False,
    )
```

time: 830 us -> 347 us (0.42)
  matrix products: 253 us -> 0 us
  Pallas kernels: 0 us -> 149 us
  waiting for transfers between devices: 247 us -> 112 us
  local copies, waits for them, and re-layouts: 127 us -> 6.72 us
  blocking collectives: 82.2 us -> 0 us
  other arithmetic: 50.8 us -> 27.6 us
  between operations: 16.2 us -> 1.16 us
    dot_general x54 -> x0, matrix products: 253 us -> none  [matrix_product(): jnp.dot(left, right, precision=lax.Precision.HIGHEST, preferred_element_t...]
    unnamed x3 -> x0, waiting for transfers between devices: 200 us -> none
    pallas_call x0 -> x5, Pallas kernels: none -> 149 us  [the longest x1 71.2 us: blocks(): pl.pallas_call(functools.partial(blocks_kernel, geo), grid=(segments,), o...]
    ppermute x16 -> x49, waiting for transfers between devices: 0.04 us -> 112 us  [the longest x42 99.8 us: swap(): lax.ppermute(value, axis, [(i, i ^ step) for i in range(lax.axis_size(axi...]
    slice x30 -> x7, local copies, waits for them, and re-layouts: 57 us -> 3.94 us  [the longest x3 1.11 us: gather_by_permutes(): b = cat([part[first:] for part in parts], 0)]
    all_gather x1 -> x0, waiting for transfers between devices: 47.1 us -> none  [body(): lax.all_gather(matrices, ('tm', 'batch'), axis=0, tiled=True)]
    unnamed x1 -> x0, blocking collectives: 42.5 us -> none
    psum x1 -> x0, blocking collectives: 39.8 us -> none  [body(): weight_sq, update_sq = lax.psum((weight_sq, update_sq), ('tm', 'batch'))]
  transfers between devices with their start and end apart: 18 -> 49, of which waited for: 2 -> 34; matrix products, arithmetic and copies ran while one was open for 10% -> 5% of each run, Pallas kernels for 0% -> 5%
where the time goes in v1:
time: 347 us; the launch traced here: 346 us
  Pallas kernels  149 us (43%)
  waiting for transfers between devices  112 us (32%)
  starting transfers between devices  49.1 us (14%)
  other arithmetic  27.6 us (8%)
  local copies, waits for them, and re-layouts  6.72 us (2%)
    ppermute x42, waiting for transfers between devices, swap(): lax.ppermute(value, axis, [(i, i ^ step) for i in range(lax.axis_size(axi...  99.8 us
    pallas_call x1, Pallas kernels, blocks(): pl.pallas_call(functools.partial(blocks_kernel, geo), grid=(segments,), o...  71.2 us
    ppermute x42, starting transfers between devices, swap(): lax.ppermute(value, axis, [(i, i ^ step) for i in range(lax.axis_size(axi...  41.3 us
    pallas_call x1, Pallas kernels, weight_back(): pl.pallas_call(functools.partial(weight_back_kernel, geo), grid=(16,), ou...  26.9 us
    pallas_call x1, Pallas kernels, prepare(): pl.pallas_call(functools.partial(prepare_kernel, geo), out_shape=(shape((...  21.9 us
    add x12, other arithmetic, scatter_by_permutes(): away.append(sum((term[slots * size:2 * slots * size] for term in part)))  18.8 us
    pallas_call x1, Pallas kernels, frames_back(): pl.pallas_call(functools.partial(frames_back_kernel, geo), grid=(16,), ou...  15.9 us
    pallas_call x1, Pallas kernels, upsample(): pl.pallas_call(functools.partial(upsample_kernel, geo), grid=(8,), out_sh...  13 us
  transfers between devices with their start and end apart: 49, of which 34 were waited for; matrix products, arithmetic and copies ran while one was open for 5% of the time, Pallas kernels for 5%

profile of v1, /device:TPU:0, one launch (start us, length us, event | category | flops | bytes accessed | tf_op | source)
XLA Modules:
  0.0 345.8 jit_solution(3606622728098694826)
XLA Ops:
  1.6 4.1 %collective-permute-start = (f32[656,128]{1,0:T(8,128)S(1)}, f32[656,128]{1,0:T(8,128)S(1)}, u32[]{:S(2)}, u32[]{:S(2)}) collective-permute-start(f32[656,128]{1,0:T(8,128)S(1)} %slice_bitcast_fusion), channel_id=1, source_target_pairs={{0,16},{8,24},{16,0},{24,8},{1,17},{9,25},{17,1},{25,9},{2,18},{10... | collective-permute-start | bytes 1007624 | tf_op jit(solution)/shard_map/ppermute | solution.py:878
  5.7 1.6 collective-permute-start.1
  9.1 2.4 collective-permute-start.4
  11.5 1.3 collective-permute-start.5
  14.6 1.6 collective-permute-start.2
  16.2 2.7 collective-permute-done.2
  18.9 1.5 collective-permute-start.3
  20.4 2.7 collective-permute-done.3
  24.3 1.6 collective-permute-start.6
  26.9 1.6 collective-permute-start.7
  28.5 2.6 collective-permute-done.7
  31.1 2.5 collective-permute-done.6
  33.8 1.6 collective-permute-start.8
  35.4 1.5 collective-permute-start.9
  36.9 2.9 collective-permute-start.10
  40.2 8.3 %collective-permute-done.10.refs_6_ = f32[448,128]{1,0:T(8,128)S(1)} collective-permute-done((f32[448,128]{1,0:T(8,128)S(1)}, f32[448,128]{1,0:T(8,128)S(1)}, u32[]{:S(2)}, u32[]{:S(2)}) %collective-permute-start.10) | collective-permute-done | bytes 229408 | tf_op jit(solution)/shard_map/ppermute | solution.py:878
  48.5 2.0 collective-permute-done.11.refs_7_
  50.7 1.5 collective-permute-start.12
  54.8 6.5 %collective-permute-done.16.refs_23_ = f32[448,128]{1,0:T(8,128)} collective-permute-done((f32[448,128]{1,0:T(8,128)S(1)}, f32[448,128]{1,0:T(8,128)}, u32[]{:S(2)}, u32[]{:S(2)}) %collective-permute-start.16) | collective-permute-done | bytes 229408 | tf_op jit(solution)/shard_map/ppermute | solution.py:878
  62.8 1.6 collective-permute-start.15
  64.4 4.5 %collective-permute-done.12.refs_19_ = f32[1312,128]{1,0:T(8,128)} collective-permute-done((f32[1312,128]{1,0:T(8,128)S(1)}, f32[1312,128]{1,0:T(8,128)}, u32[]{:S(2)}, u32[]{:S(2)}) %collective-permute-start.12) | collective-permute-done | bytes 671776 | tf_op jit(solution)/shard_map/ppermute | solution.py:878
  69.3 11.7 %collective-permute-done.14.refs_15_ = f32[1312,128]{1,0:T(8,128)} collective-permute-done((f32[1312,128]{1,0:T(8,128)S(1)}, f32[1312,128]{1,0:T(8,128)}, u32[]{:S(2)}, u32[]{:S(2)}) %collective-permute-start.14) | collective-permute-done | bytes 671776 | tf_op jit(solution)/shard_map/ppermute | solution.py:878
  81.4 1.8 collective-permute-done.21.refs_12_
  86.7 2.1 collective-permute-done.28.refs_24_
  89.0 21.9 %shard_map.194 = (bf16[16,512,256]{2,1,0:T(8,128)(2,1)}, bf16[16,512,256]{2,1,0:T(8,128)(2,1)}, bf16[3,5,256,256]{3,2,1,0:T(8,128)(2,1)}, bf16[3,5,256,256]{3,2,...) custom-call(s32[96]{0:T(128)} %concatenate.57.refs_0_, ...), custom_call_target="tpu_custom_call" | custom-call | tf_op jit(solution)/shard_map/pallas_call | solution.py:651
  110.8 13.0 %shard_map.195.start = f32[3,2,1088,128]{3,2,1,0:T(8,128)} custom-call(s32[5]{0:T(128)} %pad_add_fusion.scalars, f32[3,48,256]{2,1,0:T(8,128)} %copy-done.18, f32[3,128,512]{2,1,0:T(8,128)} %mel.5, f32[3,48,256]{2,1,0:T(8,128)} %copy-done.19, f32[16,256]{1,0:T(8,128)} %get-tuple-element.104.bias.items, ...), custom_call_target="tpu_custom_call" | custom-call | tf_op jit(solution)/shard_map/pallas_call | solution.py:693
  123.8 71.2 %shard_map.196 = (f32[3,1024,256]{2,1,0:T(8,128)}, f32[3,2,1088,128]{3,2,1,0:T(8,128)}, f32[7680,128]{1,0:T(8,128)}, f32[32,256]{1,0:T(8,128)}) custom-call(s32[5]{0:T(128)} %pad_add_fusion.scalars, f32[16,256]{1,0:T(8,128)} %get-tuple-element.104.bias.items, f32[3,2,1088,128]{3,2,1,0:T(8,128)} %shard_map.195.start, f32[3,48,256]{2,1,0:T(8,128)} %copy-done.18, ...), custom_call_target="tpu_custom_call" | custom-call | tf_op jit(solution)/shard_map/pallas_call | solution.py:727
  195.0 26.9 %shard_map.197 = (f32[5248,128]{1,0:T(8,128)}, f32[5248,128]{1,0:T(8,128)}, f32[1792,128]{1,0:T(8,128)}, f32[5248,128]{1,0:T(8,128)}, f32[5248,128]{1,0:T(8,128)}, /*index=5*/f32[1792,128]{1,0:T(8,128)}) custom-call(s32[5]{0:T(128)} %pad_add_fusion.scalars, s32[96]{0:T(128)} %concatenate.64.numbers, f32[3,128,512]{2,1,0:T(8,128)} %mel.5, ...), custom_call_target="tpu_custom_call" | custom-call | tf_op jit(solution)/shard_map/pallas_call | solution.py:779
  222.7 9.7 %collective-permute-done.31 = f32[1792,128]{1,0:T(8,128)S(1)} collective-permute-done((f32[1792,128]{1,0:T(8,128)}, f32[1792,128]{1,0:T(8,128)S(1)}, u32[]{:S(2)}, u32[]{:S(2)}) %collective-permute-start.31) | collective-permute-done | bytes 917536 | tf_op jit(solution)/shard_map/ppermute | solution.py:878
  232.4 3.5 %slice_add_fusion.1 = f32[2624,128]{1,0:T(8,128)} fusion(f32[5248,128]{1,0:T(8,128)S(1)} %collective-permute-done.29, f32[5248,128]{1,0:T(8,128)} %get-tuple-element.120), kind=kLoop, calls=%fused_computation.1 | loop fusion | flops 335872 | bytes 4030464 | tf_op jit(solution)/shard_map/add | solution.py:969
  236.5 1.3 slice_add_fusion
  239.8 15.9 %shard_map.198 = f32[3,128,512]{2,1,0:T(8,128)} custom-call(s32[5]{0:T(128)} %pad_add_fusion.scalars, f32[3,128,512]{2,1,0:T(8,128)} %mel.5, f32[3,2,1088,128]{3,2,1,0:T(8,128)} %get-tuple-element.118.back, bf16[16,512,256]{2,1,0:T(8,128)(2,1)} %get-tuple-element.107.mid_high.side_high.high, bf16[16,512,256]{2,1,0:T(8,128)(2,1)} %get-tuple-element.108.mid_low.side_low.low), custom_call_target="tpu_custom_call" | custom-call | flops 4831838208 | bytes 13303808 | tf_op jit(solution)/shard_map/pallas_call | solution.py:818
  255.7 12.1 %collective-permute-done.32 = f32[2624,128]{1,0:T(8,128)} collective-permute-done((f32[2624,128]{1,0:T(8,128)}, f32[2624,128]{1,0:T(8,128)}, u32[]{:S(2)}, u32[]{:S(2)}) %collective-permute-start.32) | collective-permute-done | bytes 1343520 | tf_op jit(solution)/shard_map/ppermute | solution.py:878
  267.8 1.5 collective-permute-done.33
  269.3 1.4 slice_add_fusion.3
  271.3 1.6 slice_add_fusion.2
  272.9 1.6 collective-permute-start.36
  275.5 2.8 collective-permute-start.37
  278.3 8.4 %collective-permute-done.37 = f32[448,128]{1,0:T(8,128)S(1)} collective-permute-done((f32[448,128]{1,0:T(8,128)S(1)}, f32[448,128]{1,0:T(8,128)S(1)}, u32[]{:S(2)}, u32[]{:S(2)}) %collective-permute-start.37) | collective-permute-done | bytes 229408 | tf_op jit(solution)/shard_map/ppermute | solution.py:878
  286.8 1.9 collective-permute-done.36
  288.7 2.2 slice_add_fusion.6
  291.5 2.0 slice_add_fusion.5
  293.5 1.3 collective-permute-start.39
  294.8 1.6 slice_add_fusion.10
  296.4 1.6 collective-permute-start.40
  298.0 3.6 %collective-permute-done.40 = f32[224,128]{1,0:T(8,128)} collective-permute-done((f32[224,128]{1,0:T(8,128)}, f32[224,128]{1,0:T(8,128)}, u32[]{:S(2)}, u32[]{:S(2)}) %collective-permute-start.40) | collective-permute-done | bytes 114720 | tf_op jit(solution)/shard_map/ppermute | solution.py:878
  302.0 4.5 %collective-permute-done.39 = f32[656,128]{1,0:T(8,128)} collective-permute-done((f32[656,128]{1,0:T(8,128)}, f32[656,128]{1,0:T(8,128)}, u32[]{:S(2)}, u32[]{:S(2)}) %collective-permute-start.39) | collective-permute-done | bytes 335904 | tf_op jit(solution)/shard_map/ppermute | solution.py:878
  306.4 1.2 slice_add_fusion.9
  307.7 3.5 %collective-permute-start.41 = (f32[328,128]{1,0:T(8,128)S(1)}, f32[328,128]{1,0:T(8,128)S(1)}, u32[]{:S(2)}, u32[]{:S(2)}) collective-permute-start(f32[328,128]{1,0:T(8,128)S(1)} %slice_add_fusion.9), channel_id=1, source_target_pairs={{0,16},{8,24},{16,0},{24,8},{1,17},{9,25},{17,1},{25,9},{2,18},{10... | collective-permute-start | bytes 503816 | tf_op jit(solution)/shard_map/ppermute | solution.py:878
  311.2 1.3 slice_add_fusion.8
  313.5 1.5 collective-permute-start.43
  315.1 2.6 collective-permute-done.43
  317.7 3.5 %collective-permute-done.41 = f32[328,128]{1,0:T(8,128)S(1)} collective-permute-done((f32[328,128]{1,0:T(8,128)S(1)}, f32[328,128]{1,0:T(8,128)S(1)}, u32[]{:S(2)}, u32[]{:S(2)}) %collective-permute-start.41) | collective-permute-done | bytes 167968 | tf_op jit(solution)/shard_map/ppermute | solution.py:878
  321.2 1.8 collective-permute-done.42
  324.0 1.3 add_add_fusion
  325.3 1.2 add_add_fusion.1
  326.6 1.1 multiply_reduce_fusion
  328.6 2.9 collective-permute-done.44
  331.5 1.2 collective-permute-start.45
  332.7 3.3 collective-permute-done.45
  335.9 1.4 collective-permute-start.46
  337.4 2.1 collective-permute-done.46
  339.5 1.5 collective-permute-start.47
  341.0 2.1 collective-permute-done.47
  (156 shorter events, 27.8 us)
Async XLA Ops:
  1.6 22.6 %collective-permute-start = (f32[656,128]{1,0:T(8,128)S(1)}, f32[656,128]{1,0:T(8,128)S(1)}, u32[]{:S(2)}, u32[]{:S(2)}) collective-permute-start(f32[656,128]{1,0:T(8,128)S(1)} %slice_bitcast_fusion), channel_id=1, source_target_pairs={{0,16},{8,24},{16,0},{24,8},{1,17},{9,25},{17,1},{25,9},{2,18},{10... | collective-permute-start | bytes 1007624 | tf_op jit(solution)/shard_map/ppermute | solution.py:878
  5.7 18.5 %collective-permute-start.1 = (f32[656,128]{1,0:T(8,128)S(1)}, f32[656,128]{1,0:T(8,128)S(1)}, u32[]{:S(2)}, u32[]{:S(2)}) collective-permute-start(f32[656,128]{1,0:T(8,128)S(1)} %slice_bitcast_fusion), channel_id=1, source_target_pairs={{0,8},{8,0},{16,24},{24,16},{1,9},{9,1},{17,25},{25,17},{2,10},{10... | collective-permute-start | bytes 1007624 | tf_op jit(solution)/shard_map/ppermute | solution.py:878
  9.1 14.2 %collective-permute-start.4 = (f32[3,48,256]{2,1,0:T(8,128)S(1)}, f32[3,48,256]{2,1,0:T(8,128)S(1)}, u32[]{:S(2)}, u32[]{:S(2)}) collective-permute-start(f32[3,48,256]{2,1,0:T(8,128)S(1)} %pad_maximum_fusion.5), channel_id=1, source_target_pairs={{0,8},{8,16},{16,24},{1,9},{9,17},{17,25},{2,10},{10,18},{18,26},{... | collective-permute-start | bytes 442376 | tf_op jit(solution)/shard_map/ppermute | solution.py:838
  11.5 12.8 %collective-permute-start.5 = (f32[3,48,256]{2,1,0:T(8,128)S(1)}, f32[3,48,256]{2,1,0:T(8,128)S(1)}, u32[]{:S(2)}, u32[]{:S(2)}) collective-permute-start(f32[3,48,256]{2,1,0:T(8,128)S(1)} %pad_maximum_fusion.6), channel_id=1, source_target_pairs={{8,0},{16,8},{24,16},{9,1},{17,9},{25,17},{10,2},{18,10},{26,18},{... | collective-permute-start | bytes 442376 | tf_op jit(solution)/shard_map/ppermute | solution.py:838
  14.6 4.2 %collective-permute-start.2 = (f32[112,128]{1,0:T(8,128)S(1)}, f32[112,128]{1,0:T(8,128)S(1)}, u32[]{:S(2)}, u32[]{:S(2)}) collective-permute-start(f32[112,128]{1,0:T(8,128)S(1)} %fusion.1), channel_id=1, source_target_pairs={{0,4},{4,0},{1,5},{5,1},{2,6},{6,2},{3,7},{7,3},{8,12},{12,8},{9,1... | collective-permute-start | bytes 172040 | tf_op jit(solution)/shard_map/ppermute | solution.py:878
  18.9 4.2 %collective-permute-start.3 = (f32[112,128]{1,0:T(8,128)S(1)}, f32[112,128]{1,0:T(8,128)S(1)}, u32[]{:S(2)}, u32[]{:S(2)}) collective-permute-start(f32[112,128]{1,0:T(8,128)S(1)} %fusion.1), channel_id=1, source_target_pairs={{0,2},{2,0},{1,3},{3,1},{4,6},{6,4},{5,7},{7,5},{8,10},{10,8},{9,1... | collective-permute-start | bytes 172040 | tf_op jit(solution)/shard_map/ppermute | solution.py:878
  24.3 9.3 %collective-permute-start.6 = (f32[656,128]{1,0:T(8,128)S(1)}, f32[656,128]{1,0:T(8,128)S(1)}, u32[]{:S(2)}, u32[]{:S(2)}) collective-permute-start(f32[656,128]{1,0:T(8,128)S(1)} %collective-permute-done), channel_id=1, source_target_pairs={{0,8},{8,0},{16,24},{24,16},{1,9},{9,1},{17,25},{25,17},{2,10},{10... | collective-permute-start | bytes 1007624 | tf_op jit(solution)/shard_map/ppermute | solution.py:878
  26.9 59.3 %copy-start.33 = (s32[1,3]{1,0:T(1,128)S(1)}, s32[1,3]{1,0:T(1,128)}, u32[]{:S(2)}) copy-start(s32[1,3]{1,0:T(1,128)} %param.12) | copy-start | bytes 40
  26.9 4.2 %collective-permute-start.7 = (f32[112,128]{1,0:T(8,128)S(1)}, f32[112,128]{1,0:T(8,128)S(1)}, u32[]{:S(2)}, u32[]{:S(2)}) collective-permute-start(f32[112,128]{1,0:T(8,128)S(1)} %collective-permute-done.2), channel_id=1, source_target_pairs={{0,2},{2,0},{1,3},{3,1},{4,6},{6,4},{5,7},{7,5},{8,10},{10,8},{9,1... | collective-permute-start | bytes 172040 | tf_op jit(solution)/shard_map/ppermute | solution.py:878
  33.6 55.2 %copy-start.7 = (f32[448,128]{1,0:T(8,128)}, f32[448,128]{1,0:T(8,128)S(1)}, u32[]{:S(2)}) copy-start(f32[448,128]{1,0:T(8,128)S(1)} %pad_maximum_fusion.4.refs_3_) | copy-start | bytes 688132
  33.7 55.2 %copy-start.1 = (f32[1312,128]{1,0:T(8,128)}, f32[1312,128]{1,0:T(8,128)S(1)}, u32[]{:S(2)}) copy-start(f32[1312,128]{1,0:T(8,128)S(1)} %pad_maximum_fusion.refs_1_) | copy-start | bytes 2015236
  33.8 55.1 %copy-start.2 = (f32[1312,128]{1,0:T(8,128)}, f32[1312,128]{1,0:T(8,128)S(1)}, u32[]{:S(2)}) copy-start(f32[1312,128]{1,0:T(8,128)S(1)} %pad_maximum_fusion.1.refs_2_) | copy-start | bytes 2015236
  33.8 16.7 %collective-permute-start.8 = (f32[1312,128]{1,0:T(8,128)S(1)}, f32[1312,128]{1,0:T(8,128)S(1)}, u32[]{:S(2)}, u32[]{:S(2)}) collective-permute-start(f32[1312,128]{1,0:T(8,128)S(1)} %pad_maximum_fusion.refs_1_), channel_id=1, source_target_pairs={{0,4},{4,0},{1,5},{5,1},{2,6},{6,2},{3,7},{7,3},{8,12},{12,8},{9,1... | collective-permute-start | bytes 2015240 | tf_op jit(solution)/shard_map/ppermute | solution.py:878
  35.4 15.2 %collective-permute-start.9 = (f32[1312,128]{1,0:T(8,128)S(1)}, f32[1312,128]{1,0:T(8,128)S(1)}, u32[]{:S(2)}, u32[]{:S(2)}) collective-permute-start(f32[1312,128]{1,0:T(8,128)S(1)} %pad_maximum_fusion.1.refs_2_), channel_id=1, source_target_pairs={{0,2},{2,0},{1,3},{3,1},{4,6},{6,4},{5,7},{7,5},{8,10},{10,8},{9,1... | collective-permute-start | bytes 2015240 | tf_op jit(solution)/shard_map/ppermute | solution.py:878
  36.9 11.6 %collective-permute-start.10 = (f32[448,128]{1,0:T(8,128)S(1)}, f32[448,128]{1,0:T(8,128)S(1)}, u32[]{:S(2)}, u32[]{:S(2)}) collective-permute-start(f32[448,128]{1,0:T(8,128)S(1)} %pad_maximum_fusion.4.refs_3_), channel_id=1, source_target_pairs={{0,16},{8,24},{16,0},{24,8},{1,17},{9,25},{17,1},{25,9},{2,18},{10... | collective-permute-start | bytes 688136 | tf_op jit(solution)/shard_map/ppermute | solution.py:878
  39.9 10.7 %collective-permute-start.11 = (f32[448,128]{1,0:T(8,128)S(1)}, f32[448,128]{1,0:T(8,128)S(1)}, u32[]{:S(2)}, u32[]{:S(2)}) collective-permute-start(f32[448,128]{1,0:T(8,128)S(1)} %pad_maximum_fusion.4.refs_3_), channel_id=1, source_target_pairs={{0,8},{8,0},{16,24},{24,16},{1,9},{9,1},{17,25},{25,17},{2,10},{10... | collective-permute-start | bytes 688136 | tf_op jit(solution)/shard_map/ppermute | solution.py:878
  48.5 40.4 %copy-start.23 = (f32[448,128]{1,0:T(8,128)}, f32[448,128]{1,0:T(8,128)S(1)}, u32[]{:S(2)}) copy-start(f32[448,128]{1,0:T(8,128)S(1)} %collective-permute-done.10.refs_6_) | copy-start | bytes 688132
  50.5 38.4 %copy-start.24 = (f32[448,128]{1,0:T(8,128)}, f32[448,128]{1,0:T(8,128)S(1)}, u32[]{:S(2)}) copy-start(f32[448,128]{1,0:T(8,128)S(1)} %collective-permute-done.11.refs_7_) | copy-start | bytes 688132
  50.5 38.4 %copy-start.10 = (f32[1312,128]{1,0:T(8,128)}, f32[1312,128]{1,0:T(8,128)S(1)}, u32[]{:S(2)}) copy-start(f32[1312,128]{1,0:T(8,128)S(1)} %collective-permute-done.8.refs_4_) | copy-start | bytes 2015236
  50.7 38.3 %copy-start.11 = (f32[1312,128]{1,0:T(8,128)}, f32[1312,128]{1,0:T(8,128)S(1)}, u32[]{:S(2)}) copy-start(f32[1312,128]{1,0:T(8,128)S(1)} %collective-permute-done.9.refs_5_) | copy-start | bytes 2015236
  50.7 18.1 %collective-permute-start.12 = (f32[1312,128]{1,0:T(8,128)S(1)}, f32[1312,128]{1,0:T(8,128)}, u32[]{:S(2)}, u32[]{:S(2)}) collective-permute-start(f32[1312,128]{1,0:T(8,128)S(1)} %collective-permute-done.8.refs_4_), channel_id=1, source_target_pairs={{0,2},{2,0},{1,3},{3,1},{4,6},{6,4},{5,7},{7,5},{8,10},{10,8},{9,1... | collective-permute-start | bytes 2015240 | tf_op jit(solution)/shard_map/ppermute | solution.py:878
  52.2 16.6 %collective-permute-start.13 = (f32[1312,128]{1,0:T(8,128)S(1)}, f32[1312,128]{1,0:T(8,128)}, u32[]{:S(2)}, u32[]{:S(2)}) collective-permute-start(f32[1312,128]{1,0:T(8,128)S(1)} %collective-permute-done.9.refs_5_), channel_id=1, source_target_pairs={{0,4},{4,0},{1,5},{5,1},{2,6},{6,2},{3,7},{7,3},{8,12},{12,8},{9,1... | collective-permute-start | bytes 2015240 | tf_op jit(solution)/shard_map/ppermute | solution.py:878
  52.7 28.4 %collective-permute-start.14 = (f32[1312,128]{1,0:T(8,128)S(1)}, f32[1312,128]{1,0:T(8,128)}, u32[]{:S(2)}, u32[]{:S(2)}) collective-permute-start(f32[1312,128]{1,0:T(8,128)S(1)} %pad_maximum_fusion.refs_1_), channel_id=1, source_target_pairs={{0,2},{2,0},{1,3},{3,1},{4,6},{6,4},{5,7},{7,5},{8,10},{10,8},{9,1... | collective-permute-start | bytes 2015240 | tf_op jit(solution)/shard_map/ppermute | solution.py:878
  53.2 1.5 collective-permute-start.19
  53.2 8.1 %collective-permute-start.16 = (f32[448,128]{1,0:T(8,128)S(1)}, f32[448,128]{1,0:T(8,128)}, u32[]{:S(2)}, u32[]{:S(2)}) collective-permute-start(f32[448,128]{1,0:T(8,128)S(1)} %collective-permute-done.10.refs_6_), channel_id=1, source_target_pairs={{0,8},{8,0},{16,24},{24,16},{1,9},{9,1},{17,25},{25,17},{2,10},{10... | collective-permute-start | bytes 688136 | tf_op jit(solution)/shard_map/ppermute | solution.py:878
  54.7 6.6 %collective-permute-start.22 = (f32[448,128]{1,0:T(8,128)S(1)}, f32[448,128]{1,0:T(8,128)}, u32[]{:S(2)}, u32[]{:S(2)}) collective-permute-start(f32[448,128]{1,0:T(8,128)S(1)} %collective-permute-done.10.refs_6_), channel_id=1, source_target_pairs={{0,1},{1,0},{2,3},{3,2},{4,5},{5,4},{6,7},{7,6},{8,9},{9,8},{10,11... | collective-permute-start | bytes 688136 | tf_op jit(solution)/shard_map/ppermute | solution.py:878
  61.3 1.5 collective-permute-start.23
  61.3 20.0 %collective-permute-start.17 = (f32[1312,128]{1,0:T(8,128)S(1)}, f32[1312,128]{1,0:T(8,128)S(1)}, u32[]{:S(2)}, u32[]{:S(2)}) collective-permute-start(f32[1312,128]{1,0:T(8,128)S(1)} %pad_maximum_fusion.refs_1_), channel_id=1, source_target_pairs={{0,1},{1,0},{2,3},{3,2},{4,5},{5,4},{6,7},{7,6},{8,9},{9,8},{10,11... | collective-permute-start | bytes 2015240 | tf_op jit(solution)/shard_map/ppermute | solution.py:878
  62.8 18.5 %collective-permute-start.15 = (f32[1312,128]{1,0:T(8,128)S(1)}, f32[1312,128]{1,0:T(8,128)}, u32[]{:S(2)}, u32[]{:S(2)}) collective-permute-start(f32[1312,128]{1,0:T(8,128)S(1)} %pad_maximum_fusion.1.refs_2_), channel_id=1, source_target_pairs={{0,4},{4,0},{1,5},{5,1},{2,6},{6,2},{3,7},{7,3},{8,12},{12,8},{9,1... | collective-permute-start | bytes 2015240 | tf_op jit(solution)/shard_map/ppermute | solution.py:878
  68.8 12.5 %collective-permute-start.18 = (f32[1312,128]{1,0:T(8,128)S(1)}, f32[1312,128]{1,0:T(8,128)S(1)}, u32[]{:S(2)}, u32[]{:S(2)}) collective-permute-start(f32[1312,128]{1,0:T(8,128)S(1)} %pad_maximum_fusion.1.refs_2_), channel_id=1, source_target_pairs={{0,1},{1,0},{2,3},{3,2},{4,5},{5,4},{6,7},{7,6},{8,9},{9,8},{10,11... | collective-permute-start | bytes 2015240 | tf_op jit(solution)/shard_map/ppermute | solution.py:878
  68.8 12.5 %collective-permute-start.20 = (f32[1312,128]{1,0:T(8,128)S(1)}, f32[1312,128]{1,0:T(8,128)S(1)}, u32[]{:S(2)}, u32[]{:S(2)}) collective-permute-start(f32[1312,128]{1,0:T(8,128)S(1)} %collective-permute-done.8.refs_4_), channel_id=1, source_target_pairs={{0,1},{1,0},{2,3},{3,2},{4,5},{5,4},{6,7},{7,6},{8,9},{9,8},{10,11... | collective-permute-start | bytes 2015240 | tf_op jit(solution)/shard_map/ppermute | solution.py:878
  81.1 2.1 collective-permute-start.21
  83.2 5.7 %collective-permute-start.24 = (f32[1312,128]{1,0:T(8,128)}, f32[1312,128]{1,0:T(8,128)}, u32[]{:S(2)}, u32[]{:S(2)}) collective-permute-start(f32[1312,128]{1,0:T(8,128)} %collective-permute-done.14.refs_15_), channel_id=1, source_target_pairs={{0,1},{1,0},{2,3},{3,2},{4,5},{5,4},{6,7},{7,6},{8,9},{9,8},{10,11... | collective-permute-start | bytes 2015240 | tf_op jit(solution)/shard_map/ppermute | solution.py:878
  83.3 5.5 %collective-permute-start.25 = (f32[1312,128]{1,0:T(8,128)}, f32[1312,128]{1,0:T(8,128)}, u32[]{:S(2)}, u32[]{:S(2)}) collective-permute-start(f32[1312,128]{1,0:T(8,128)} %collective-permute-done.15.refs_17_), channel_id=1, source_target_pairs={{0,1},{1,0},{2,3},{3,2},{4,5},{5,4},{6,7},{7,6},{8,9},{9,8},{10,11... | collective-permute-start | bytes 2015240 | tf_op jit(solution)/shard_map/ppermute | solution.py:878
  83.7 5.2 %collective-permute-start.26 = (f32[1312,128]{1,0:T(8,128)}, f32[1312,128]{1,0:T(8,128)}, u32[]{:S(2)}, u32[]{:S(2)}) collective-permute-start(f32[1312,128]{1,0:T(8,128)} %collective-permute-done.12.refs_19_), channel_id=1, source_target_pairs={{0,1},{1,0},{2,3},{3,2},{4,5},{5,4},{6,7},{7,6},{8,9},{9,8},{10,11... | collective-permute-start | bytes 2015240 | tf_op jit(solution)/shard_map/ppermute | solution.py:878
  84.1 4.8 %collective-permute-start.27 = (f32[1312,128]{1,0:T(8,128)}, f32[1312,128]{1,0:T(8,128)}, u32[]{:S(2)}, u32[]{:S(2)}) collective-permute-start(f32[1312,128]{1,0:T(8,128)} %collective-permute-done.13.refs_21_), channel_id=1, source_target_pairs={{0,1},{1,0},{2,3},{3,2},{4,5},{5,4},{6,7},{7,6},{8,9},{9,8},{10,11... | collective-permute-start | bytes 2015240 | tf_op jit(solution)/shard_map/ppermute | solution.py:878
  84.2 4.6 %collective-permute-start.28 = (f32[448,128]{1,0:T(8,128)}, f32[448,128]{1,0:T(8,128)}, u32[]{:S(2)}, u32[]{:S(2)}) collective-permute-start(f32[448,128]{1,0:T(8,128)} %collective-permute-done.16.refs_23_), channel_id=1, source_target_pairs={{0,1},{1,0},{2,3},{3,2},{4,5},{5,4},{6,7},{7,6},{8,9},{9,8},{10,11... | collective-permute-start | bytes 688136 | tf_op jit(solution)/shard_map/ppermute | solution.py:878
  221.9 14.6 %copy-start.4 = (f32[5248,128]{1,0:T(8,128)S(1)}, f32[5248,128]{1,0:T(8,128)}, u32[]{:S(2)}) copy-start(f32[5248,128]{1,0:T(8,128)} %get-tuple-element.125) | copy-start | bytes 8060932
  221.9 10.4 %collective-permute-start.29 = (f32[5248,128]{1,0:T(8,128)}, f32[5248,128]{1,0:T(8,128)S(1)}, u32[]{:S(2)}, u32[]{:S(2)}) collective-permute-start(f32[5248,128]{1,0:T(8,128)} %get-tuple-element.121), channel_id=1, source_target_pairs={{0,1},{1,0},{2,3},{3,2},{4,5},{5,4},{6,7},{7,6},{8,9},{9,8},{10,11... | collective-permute-start | bytes 8060936 | tf_op jit(solution)/shard_map/ppermute | solution.py:878
  222.1 10.2 %collective-permute-start.30 = (f32[5248,128]{1,0:T(8,128)}, f32[5248,128]{1,0:T(8,128)S(1)}, u32[]{:S(2)}, u32[]{:S(2)}) collective-permute-start(f32[5248,128]{1,0:T(8,128)} %get-tuple-element.122), channel_id=1, source_target_pairs={{0,1},{1,0},{2,3},{3,2},{4,5},{5,4},{6,7},{7,6},{8,9},{9,8},{10,11... | collective-permute-start | bytes 8060936 | tf_op jit(solution)/shard_map/ppermute | solution.py:878
  222.5 9.9 %collective-permute-start.31 = (f32[1792,128]{1,0:T(8,128)}, f32[1792,128]{1,0:T(8,128)S(1)}, u32[]{:S(2)}, u32[]{:S(2)}) collective-permute-start(f32[1792,128]{1,0:T(8,128)} %get-tuple-element.123), channel_id=1, source_target_pairs={{0,1},{1,0},{2,3},{3,2},{4,5},{5,4},{6,7},{7,6},{8,9},{9,8},{10,11... | collective-permute-start | bytes 2752520 | tf_op jit(solution)/shard_map/ppermute | solution.py:878
  235.9 31.9 %collective-permute-start.32 = (f32[2624,128]{1,0:T(8,128)}, f32[2624,128]{1,0:T(8,128)}, u32[]{:S(2)}, u32[]{:S(2)}) collective-permute-start(f32[2624,128]{1,0:T(8,128)} %slice_add_fusion.1), channel_id=1, source_target_pairs={{0,2},{2,0},{1,3},{3,1},{4,6},{6,4},{5,7},{7,5},{8,10},{10,8},{9,1... | collective-permute-start | bytes 4030472 | tf_op jit(solution)/shard_map/ppermute | solution.py:878
  237.8 31.6 %collective-permute-start.33 = (f32[2624,128]{1,0:T(8,128)}, f32[2624,128]{1,0:T(8,128)}, u32[]{:S(2)}, u32[]{:S(2)}) collective-permute-start(f32[2624,128]{1,0:T(8,128)} %slice_add_fusion), channel_id=1, source_target_pairs={{0,4},{4,0},{1,5},{5,1},{2,6},{6,2},{3,7},{7,3},{8,12},{12,8},{9,1... | collective-permute-start | bytes 4030472 | tf_op jit(solution)/shard_map/ppermute | solution.py:878
  239.1 30.2 %copy-start.3 = (f32[5248,128]{1,0:T(8,128)S(1)}, f32[5248,128]{1,0:T(8,128)}, u32[]{:S(2)}) copy-start(f32[5248,128]{1,0:T(8,128)} %get-tuple-element.120) | copy-start | bytes 8060932
  239.1 16.6 %collective-permute-start.34 = (f32[896,128]{1,0:T(8,128)}, f32[896,128]{1,0:T(8,128)S(1)}, u32[]{:S(2)}, u32[]{:S(2)}) collective-permute-start(f32[896,128]{1,0:T(8,128)} %slice_add_fusion.4), channel_id=1, source_target_pairs={{0,8},{8,0},{16,24},{24,16},{1,9},{9,1},{17,25},{25,17},{2,10},{10... | collective-permute-start | bytes 1376264 | tf_op jit(solution)/shard_map/ppermute | solution.py:878
  270.7 16.0 %collective-permute-start.35 = (f32[1312,128]{1,0:T(8,128)S(1)}, f32[1312,128]{1,0:T(8,128)S(1)}, u32[]{:S(2)}, u32[]{:S(2)}) collective-permute-start(f32[1312,128]{1,0:T(8,128)S(1)} %slice_add_fusion.3), channel_id=1, source_target_pairs={{0,4},{4,0},{1,5},{5,1},{2,6},{6,2},{3,7},{7,3},{8,12},{12,8},{9,1... | collective-permute-start | bytes 2015240 | tf_op jit(solution)/shard_map/ppermute | solution.py:878
  272.9 15.8 %collective-permute-start.36 = (f32[1312,128]{1,0:T(8,128)S(1)}, f32[1312,128]{1,0:T(8,128)S(1)}, u32[]{:S(2)}, u32[]{:S(2)}) collective-permute-start(f32[1312,128]{1,0:T(8,128)S(1)} %slice_add_fusion.2), channel_id=1, source_target_pairs={{0,2},{2,0},{1,3},{3,1},{4,6},{6,4},{5,7},{7,5},{8,10},{10,8},{9,1... | collective-permute-start | bytes 2015240 | tf_op jit(solution)/shard_map/ppermute | solution.py:878
  275.5 11.2 %collective-permute-start.37 = (f32[448,128]{1,0:T(8,128)S(1)}, f32[448,128]{1,0:T(8,128)S(1)}, u32[]{:S(2)}, u32[]{:S(2)}) collective-permute-start(f32[448,128]{1,0:T(8,128)S(1)} %slice_add_fusion.7), channel_id=1, source_target_pairs={{0,16},{8,24},{16,0},{24,8},{1,17},{9,25},{17,1},{25,9},{2,18},{10... | collective-permute-start | bytes 688136 | tf_op jit(solution)/shard_map/ppermute | solution.py:878
  290.8 24.1 %copy-start.27 = (f32[16,128]{1,0:T(8,128)S(1)}, f32[16,128]{1,0:T(8,128)}, u32[]{:S(2)}) copy-start(f32[16,128]{1,0:T(8,128)} %get-tuple-element.130) | copy-start | bytes 24580
  290.8 11.1 %collective-permute-start.38 = (f32[656,128]{1,0:T(8,128)}, f32[656,128]{1,0:T(8,128)}, u32[]{:S(2)}, u32[]{:S(2)}) collective-permute-start(f32[656,128]{1,0:T(8,128)} %slice_add_fusion.6), channel_id=1, source_target_pairs={{0,8},{8,0},{16,24},{24,16},{1,9},{9,1},{17,25},{25,17},{2,10},{10... | collective-permute-start | bytes 1007624 | tf_op jit(solution)/shard_map/ppermute | solution.py:878
  293.5 13.0 %collective-permute-start.39 = (f32[656,128]{1,0:T(8,128)}, f32[656,128]{1,0:T(8,128)}, u32[]{:S(2)}, u32[]{:S(2)}) collective-permute-start(f32[656,128]{1,0:T(8,128)} %slice_add_fusion.5), channel_id=1, source_target_pairs={{0,8},{8,0},{16,24},{24,16},{1,9},{9,1},{17,25},{25,17},{2,10},{10... | collective-permute-start | bytes 1007624 | tf_op jit(solution)/shard_map/ppermute | solution.py:878
  296.4 30.1 %copy-start = (f32[96256]{0:T(1024)S(1)}, f32[96256]{0:T(1024)}, u32[]{:S(2)}) copy-start(f32[96256]{0:T(1024)} %param.14) | copy-start | bytes 1155076
  296.4 5.2 %collective-permute-start.40 = (f32[224,128]{1,0:T(8,128)}, f32[224,128]{1,0:T(8,128)}, u32[]{:S(2)}, u32[]{:S(2)}) collective-permute-start(f32[224,128]{1,0:T(8,128)} %slice_add_fusion.10), channel_id=1, source_target_pairs={{0,2},{2,0},{1,3},{3,1},{4,6},{6,4},{5,7},{7,5},{8,10},{10,8},{9,1... | collective-permute-start | bytes 344072 | tf_op jit(solution)/shard_map/ppermute | solution.py:878
  298.0 28.6 %copy-start.20 = (f32[96256]{0:T(1024)S(1)}, f32[96256]{0:T(1024)}, u32[]{:S(2)}) copy-start(f32[96256]{0:T(1024)} %param.17) | copy-start | bytes 1155076
  298.0 28.6 %copy-start.21 = (f32[96256]{0:T(1024)S(1)}, f32[96256]{0:T(1024)}, u32[]{:S(2)}) copy-start(f32[96256]{0:T(1024)} %param.16) | copy-start | bytes 1155076
  307.7 13.6 %collective-permute-start.41 = (f32[328,128]{1,0:T(8,128)S(1)}, f32[328,128]{1,0:T(8,128)S(1)}, u32[]{:S(2)}, u32[]{:S(2)}) collective-permute-start(f32[328,128]{1,0:T(8,128)S(1)} %slice_add_fusion.9), channel_id=1, source_target_pairs={{0,16},{8,24},{16,0},{24,8},{1,17},{9,25},{17,1},{25,9},{2,18},{10... | collective-permute-start | bytes 503816 | tf_op jit(solution)/shard_map/ppermute | solution.py:878
  312.5 10.6 %collective-permute-start.42 = (f32[328,128]{1,0:T(8,128)S(1)}, f32[328,128]{1,0:T(8,128)S(1)}, u32[]{:S(2)}, u32[]{:S(2)}) collective-permute-start(f32[328,128]{1,0:T(8,128)S(1)} %slice_add_fusion.8), channel_id=1, source_target_pairs={{0,16},{8,24},{16,0},{24,8},{1,17},{9,25},{17,1},{25,9},{2,18},{10... | collective-permute-start | bytes 503816 | tf_op jit(solution)/shard_map/ppermute | solution.py:878
  313.5 4.2 %collective-permute-start.43 = (f32[112,128]{1,0:T(8,128)S(1)}, f32[112,128]{1,0:T(8,128)S(1)}, u32[]{:S(2)}, u32[]{:S(2)}) collective-permute-start(f32[112,128]{1,0:T(8,128)S(1)} %slice_add_fusion.11), channel_id=1, source_target_pairs={{0,4},{4,0},{1,5},{5,1},{2,6},{6,2},{3,7},{7,3},{8,12},{12,8},{9,1... | collective-permute-start | bytes 172040 | tf_op jit(solution)/shard_map/ppermute | solution.py:878
  315.1 12.9 %copy-start.30 = (f32[120]{0:T(128)S(1)}, f32[120]{0:T(128)}, u32[]{:S(2)}) copy-start(f32[120]{0:T(128)} %param.15) | copy-start | bytes 1444
  327.9 3.6 %collective-permute-start.44 = (f32[10]{0:T(128)S(1)}, f32[10]{0:T(128)S(1)}, u32[]{:S(2)}, u32[]{:S(2)}) collective-permute-start(f32[10]{0:T(128)S(1)} %select_reduce_fusion.1), channel_id=1, source_target_pairs={{0,8},{8,0},{16,24},{24,16},{1,9},{9,1},{17,25},{25,17},{2,10},{10... | collective-permute-start | bytes 128 | tf_op jit(solution)/shard_map/ppermute | solution.py:866
  331.5 4.4 %collective-permute-start.45 = (f32[10]{0:T(128)S(1)}, f32[10]{0:T(128)S(1)}, u32[]{:S(2)}, u32[]{:S(2)}) collective-permute-start(f32[10]{0:T(128)S(1)} %add.720), channel_id=1, source_target_pairs={{0,16},{8,24},{16,0},{24,8},{1,17},{9,25},{17,1},{25,9},{2,18},{10... | collective-permute-start | bytes 128 | tf_op jit(solution)/shard_map/ppermute | solution.py:866
  335.9 3.5 %collective-permute-start.46 = (f32[10]{0:T(128)S(1)}, f32[10]{0:T(128)S(1)}, u32[]{:S(2)}, u32[]{:S(2)}) collective-permute-start(f32[10]{0:T(128)S(1)} %add.721), channel_id=1, source_target_pairs={{0,4},{4,0},{1,5},{5,1},{2,6},{6,2},{3,7},{7,3},{8,12},{12,8},{9,1... | collective-permute-start | bytes 128 | tf_op jit(solution)/shard_map/ppermute | solution.py:866
  339.5 3.5 %collective-permute-start.47 = (f32[10]{0:T(128)S(1)}, f32[10]{0:T(128)S(1)}, u32[]{:S(2)}, u32[]{:S(2)}) collective-permute-start(f32[10]{0:T(128)S(1)} %add.722), channel_id=1, source_target_pairs={{0,2},{2,0},{1,3},{3,1},{4,6},{6,4},{5,7},{7,5},{8,10},{10,8},{9,1... | collective-permute-start | bytes 128 | tf_op jit(solution)/shard_map/ppermute | solution.py:866
  343.0 1.1 collective-permute-start.48
  (19 other events, 132.5 us)
